TPU v7x, 128 devices: a whole 4x4x4 slice. The times are simulated.
128 devices in a mesh: seq: 32 (over z, x, core), tp: 4 (over y).
Axes of the slice: x: 4, y: 4, z: 4, core: 2. Of those that a mesh axis runs over, the one named last changes fastest.
Arguments:
- tokens: bfloat16 [131072, 1024], P('seq'), may hold values from -16 to 16
- w_qkv: bfloat16 [3, 1024, 1024], P(None, None, 'tp'), as said below
- w_out: bfloat16 [1024, 1024], P('tp'), may hold values from -0.1875 to 0.1875
Outputs:
- mixed: bfloat16 [131072, 1024], P('seq', 'tp')
Inputs may be any that keep to these rules, and one draw needn't show every extreme that they name: `w_qkv`: entries lie within six times 1024 ** -0.5 of zero.
All inputs are finite; a program needn't handle non-finite values.
Results may differ from a plain program's by a relative error of at most 0.03.
Values may be sent and summed in bfloat16 or wider, within the bound.
A program may use at most 128 MiB of HBM per device.

v0:
```python
import functools

import jax
import jax.numpy as jnp
from jax import lax
from jax.sharding import Mesh
from jax.sharding import PartitionSpec as P

HEAD_DIM = 64
LANDMARKS = 256
NEWTON = 6
SEQ = ("seq_0", "seq_1", "seq_2")


def in_order(parts, dim):
    dims = list(parts.shape[1:])
    dims[dim] *= parts.shape[0]
    return jnp.moveaxis(parts, 0, dim).reshape(dims)


def gather_together(arrays, axis, dims):
    flat = jnp.concatenate([a.reshape(-1) for a in arrays])
    lines, at, finished = (lax.all_gather(flat, axis), 0, [])
    for a, dim in zip(arrays, dims):
        parts = lines[:, at : at + a.size].reshape(-1, *a.shape)
        finished.append(in_order(parts, dim))
        at += a.size
    return tuple(finished)


def one_axis_at_a_time(shard, axes):
    return functools.reduce(lax.pmax, axes, shard)


def in_one(arrays, axis):
    ends = [0]
    for a in arrays:
        ends.append(ends[-1] + a.size)
    running = lax.psum(jnp.concatenate([a.ravel() for a in arrays]), axis)
    return tuple((running[b:e].reshape(a.shape) for a, b, e in zip(arrays, ends, ends[1:])))


def softmax_rows(logit_scores):
    top = jnp.max(logit_scores, axis=-1, keepdims=True)
    exponent_terms = jnp.exp(logit_scores - top)
    return exponent_terms / jnp.sum(exponent_terms, axis=-1, keepdims=True)


def newton_inverse(kernel_a):
    hi = lax.Precision.HIGHEST
    eye = jnp.eye(kernel_a.shape[-1], dtype=jnp.float32)[None]
    colmax = jnp.max(jnp.sum(kernel_a, axis=1), axis=1)
    rowmax = jnp.max(jnp.sum(kernel_a, axis=2), axis=1)
    approx = jnp.transpose(kernel_a, (0, 2, 1)) / (colmax * rowmax)[:, None, None]
    for turn in range(NEWTON):
        prod_az = jnp.einsum("hij,hjk->hik", kernel_a, approx, precision=hi)
        inner = jnp.einsum("hij,hjk->hik", prod_az, 7.0 * eye - prod_az, precision=hi)
        outer = jnp.einsum("hij,hjk->hik", prod_az, 15.0 * eye - inner, precision=hi)
        approx = 0.25 * jnp.einsum("hij,hjk->hik", approx, 13.0 * eye - outer, precision=hi)
    return approx


def on_device(tokens, w_qkv, w_out):
    width = w_out.shape[0]
    heads = width // HEAD_DIM
    count = tokens.shape[0]
    local_marks = LANDMARKS // lax.axis_size(SEQ)
    segment = count // local_marks
    score_scale = HEAD_DIM ** (-0.5)
    proj = jnp.einsum("td,cde->cte", tokens, w_qkv, preferred_element_type=jnp.float32).astype(
        jnp.bfloat16
    )
    queries, keys, values = (proj[0], proj[1], proj[2])

    def marks(array):
        return jnp.mean(
            array.astype(jnp.float32).reshape(local_marks, segment, width), axis=1
        ).astype(jnp.bfloat16)

    q_marks, k_marks = gather_together((marks(queries), marks(keys)), SEQ, (0, 0))
    query_per_head = queries.reshape(count, heads, HEAD_DIM)
    key_per_head = keys.reshape(count, heads, HEAD_DIM)
    value_per_head = values.reshape(count, heads, HEAD_DIM)
    query_landmark_rows = q_marks.reshape(LANDMARKS, heads, HEAD_DIM)
    key_landmark_rows = k_marks.reshape(LANDMARKS, heads, HEAD_DIM)
    kernel_a = softmax_rows(
        jnp.einsum(
            "oyc,wyc->yow",
            query_landmark_rows,
            key_landmark_rows,
            preferred_element_type=jnp.float32,
        )
        * score_scale
    )
    pseudoinverse_kernel = newton_inverse(kernel_a)
    query_kernel_matrix = softmax_rows(
        jnp.einsum(
            "vse,zse->svz", query_per_head, key_landmark_rows, preferred_element_type=jnp.float32
        )
        * score_scale
    ).astype(jnp.bfloat16)
    logit_scores = (
        jnp.einsum(
            "bzx,gzx->zbg", query_landmark_rows, key_per_head, preferred_element_type=jnp.float32
        )
        * score_scale
    )
    block_max = jnp.max(logit_scores, axis=-1)
    exponent_terms = jnp.exp(logit_scores - block_max[:, :, None])
    block_total = jnp.sum(exponent_terms, axis=-1)
    block_acc = jnp.einsum(
        "luj,jlc->luc",
        exponent_terms.astype(jnp.bfloat16),
        value_per_head,
        preferred_element_type=jnp.float32,
    )
    row_max = one_axis_at_a_time(block_max, SEQ)
    factor = jnp.exp(block_max - row_max)
    total, summed = tuple(
        (
            part.astype(jnp.float32)
            for part in in_one(
                (
                    (block_total * factor).astype(jnp.bfloat16),
                    (block_acc * factor[:, :, None]).astype(jnp.bfloat16),
                ),
                SEQ,
            )
        )
    )
    landmark_value_rows = summed / total[:, :, None]
    center_kernel = jnp.einsum(
        "ole,oer->olr", pseudoinverse_kernel, landmark_value_rows, precision=lax.Precision.HIGHEST
    ).astype(jnp.bfloat16)
    attended = (
        jnp.einsum(
            "cye,cea->yca", query_kernel_matrix, center_kernel, preferred_element_type=jnp.float32
        )
        .astype(jnp.bfloat16)
        .reshape(count, width)
    )
    partial_out = jnp.dot(attended, w_out, preferred_element_type=jnp.float32)
    mixed = lax.psum_scatter(
        partial_out.astype(jnp.bfloat16), "tp", scatter_dimension=1, tiled=True
    )
    return mixed


def solution(mesh):
    split = Mesh(mesh.devices.reshape(4, 4, 2, mesh.shape["tp"]), ("seq_0", "seq_1", "seq_2", "tp"))
    placed = (P(SEQ, None), P(None, None, "tp"), P("tp", None))
    return jax.shard_map(
        on_device, mesh=split, in_specs=placed, out_specs=P(SEQ, "tp"), check_vma=False
    )
```

profile of v0, /device:TPU:1, one launch (start us, length us, event | category | flops | bytes accessed | tf_op | source)
XLA Modules:
  0.0 319.2 jit_solution(16555199662229192901)
XLA Ops:
  6.5 1.4 copy-done
  7.9 10.9 %fusion.16 = bf16[3,4096,256]{1,2,0:T(8,128)(2,1)S(1)} fusion(bf16[3,1024,256]{2,1,0:T(8,128)(2,1)S(1)} %copy-done, bf16[4096,1024]{1,0:T(8,128)(2,1)} %param.3), kind=kOutput, calls=%fused_computation.17 | convolution fusion | flops 6445596672 | bytes 16252928 | tf_op jit(solution)/shard_map/td,cde->cte/dot_general | solution.py:70
  18.9 4.6 %fusion.79 = (bf16[1,4096,256]{1,2,0:T(8,128)(2,1)}, f32[1,4096,256]{1,2,0:T(8,128)S(1)}, f32[1,4096,256]{1,2,0:T(8,128)}, bf16[1,4096,256]{1,2,0:T(8,128)(2,1)}, bf16[1,4096,256]{1,2,0:T(8,128)(2,1)}) fusion(bf16[3,4096,256]{1,2,0:T(8,128)(2,1)S(1)} %fusion.16), kind=kLoop, calls=%fused_computation.88 | loop fusion | flops 2097152 | bytes 20971520 | tf_op jit(solution)/shard_map/slice | solution.py:73
  23.4 5.8 %copy.74 = f32[32,8,8,512]{3,2,1,0:T(8,128)} copy(f32[32,8,8,512]{3,1,2,0:T(8,128)S(1)} %bitcast.83) | data formatting | bytes 8388608
  29.2 2.5 reduce_sum.63
  31.8 8.0 %copy.76 = f32[32,8,8,512]{3,2,1,0:T(8,128)} copy(f32[32,8,8,512]{3,1,2,0:T(8,128)} %bitcast.82) | data formatting | bytes 8388608
  39.8 2.5 reduce_sum.64
  42.4 28.0 %all-gather = bf16[131072]{0:T(1024)(128)(2,1)S(1)} all-gather(bf16[4096]{0:T(1024)(128)(2,1)S(1)} %pad_maximum_fusion.1), channel_id=2, replica_groups=mesh['seq_0'=4,'seq_1'=4,'seq_2'=2,'tp'=4] {'seq_0','seq_1','seq_2'}, dimensions={0}, use_global_device_ids=true | all-gather | bytes 270336 | tf_op jit(solution)/shard_map/all_gather | solution.py:23
  71.0 9.7 %multiply_reduce_fusion = (f32[4,256]{1,0:T(4,128)S(1)}, f32[4,256,4096]{2,1,0:T(8,128)}) fusion(bf16[256,4,64]{0,2,1:T(8,128)(2,1)S(1)} %copy.59, bf16[4096,4,64]{0,2,1:T(8,128)(2,1)} %bitcast.87), kind=kOutput, calls=%fused_computation.5 | convolution fusion | flops 545258496 | bytes 19009536 | tf_op jit(solution)/shard_map/bzx,gzx->zbg/dot_general | solution.py:103
  80.6 8.1 %pmax.21 = f32[4,256]{1,0:T(4,128)S(1)} all-reduce(f32[4,256]{1,0:T(4,128)S(1)} %get-tuple-element.18), channel_id=1, replica_groups=mesh['seq_0'=4,'seq_1'=4,'seq_2'=2,'tp'=4] {'seq_0'}, use_global_device_ids=true, to_apply=%region_10.0 | all-reduce | flops 1024 | bytes 8192 | tf_op jit(solution)/shard_map/pmax | solution.py:32
  88.7 8.6 %fusion.4 = f32[4,256]{1,0:T(4,128)S(1)} fusion(f32[4,256,4096]{2,1,0:T(8,128)} %get-tuple-element.19, f32[4,256]{1,0:T(4,128)S(1)} %get-tuple-element.18), kind=kLoop, calls=%fused_computation.9 | loop fusion | flops 12581888 | bytes 16785408 | tf_op jit(solution)/shard_map/reduce_sum | solution.py:110
  97.3 6.5 %pmax.22 = f32[4,256]{1,0:T(4,128)S(1)} all-reduce(f32[4,256]{1,0:T(4,128)S(1)} %pmax.21), channel_id=1, replica_groups=mesh['seq_0'=4,'seq_1'=4,'seq_2'=2,'tp'=4] {'seq_1'}, use_global_device_ids=true, to_apply=%region_11.0 | all-reduce | flops 1024 | bytes 8192 | tf_op jit(solution)/shard_map/pmax | solution.py:32
  103.9 6.3 %pmax.23 = f32[4,256]{1,0:T(4,128)S(1)} all-reduce(f32[4,256]{1,0:T(4,128)S(1)} %pmax.22), channel_id=1, replica_groups=mesh['seq_0'=4,'seq_1'=4,'seq_2'=2,'tp'=4] {'seq_2'}, use_global_device_ids=true, to_apply=%region_12.0 | all-reduce | flops 1024 | bytes 8192 | tf_op jit(solution)/shard_map/pmax | solution.py:32
  110.2 9.4 %fusion.55 = bf16[4,256,64]{1,2,0:T(8,128)(2,1)S(1)} fusion(bf16[4096,4,64]{0,2,1:T(8,128)(2,1)} %bitcast.86, f32[4,256,4096]{2,1,0:T(8,128)} %get-tuple-element.19, f32[4,256]{1,0:T(4,128)S(1)} %get-tuple-element.18, f32[4,256]{1,0:T(4,128)S(1)} %get-tuple-element.8), kind=kOutput, calls=%fused_computation.53 | convolution fusion | flops 549584896 | bytes 19013632 | tf_op jit(solution)/shard_map/luj,jlc->luc/dot_general | solution.py:111
  122.0 1.3 convolution_multiply_fusion.6
  124.1 1.3 bitcast_divide_fusion
  125.3 2.6 copy.62
  128.0 4.6 %online-softmax = f32[4,256,256]{2,1,0:T(8,128)} custom-call(f32[4,256,256]{2,1,0:T(8,128)} %convolution_multiply_fusion.6, f32[4,256,256]{2,1,0:T(8,128)} %copy.62), custom_call_target="tpu_custom_call" | custom-call | tf_op online-softmax
  132.6 2.7 fusion.34
  135.4 2.4 convolution_subtract_fusion.5
  137.8 2.9 convolution_multiply_fusion.5
  140.7 4.8 %online-softmax.1 = f32[4,256,256]{2,1,0:T(8,128)} custom-call(f32[4,256,256]{2,1,0:T(8,128)} %convolution_multiply_fusion.6, f32[4,256,256]{2,1,0:T(8,128)} %convolution_multiply_fusion.5), custom_call_target="tpu_custom_call" | custom-call | tf_op online-softmax
  145.4 2.7 fusion.37
  148.2 2.4 convolution_subtract_fusion.4
  150.6 2.2 convolution_multiply_fusion.4
  152.7 4.9 %online-softmax.2 = f32[4,256,256]{2,1,0:T(8,128)} custom-call(f32[4,256,256]{2,1,0:T(8,128)} %convolution_multiply_fusion.6, f32[4,256,256]{2,1,0:T(8,128)} %convolution_multiply_fusion.4), custom_call_target="tpu_custom_call" | custom-call | tf_op online-softmax
  157.7 2.7 fusion.40
  160.4 2.4 convolution_subtract_fusion.3
  162.8 2.2 convolution_multiply_fusion.3
  165.0 4.7 %online-softmax.3 = f32[4,256,256]{2,1,0:T(8,128)} custom-call(f32[4,256,256]{2,1,0:T(8,128)} %convolution_multiply_fusion.6, f32[4,256,256]{2,1,0:T(8,128)} %convolution_multiply_fusion.3), custom_call_target="tpu_custom_call" | custom-call | tf_op online-softmax
  169.8 2.7 fusion.43
  172.5 2.4 convolution_subtract_fusion.2
  174.9 2.2 convolution_multiply_fusion.2
  177.1 4.8 %online-softmax.4 = f32[4,256,256]{2,1,0:T(8,128)} custom-call(f32[4,256,256]{2,1,0:T(8,128)} %convolution_multiply_fusion.6, f32[4,256,256]{2,1,0:T(8,128)} %convolution_multiply_fusion.2), custom_call_target="tpu_custom_call" | custom-call | tf_op online-softmax
  181.8 2.7 fusion.46
  184.6 2.4 convolution_subtract_fusion.1
  187.0 2.1 convolution_multiply_fusion.1
  189.1 4.9 %online-softmax.5 = f32[4,256,256]{2,1,0:T(8,128)} custom-call(f32[4,256,256]{2,1,0:T(8,128)} %convolution_multiply_fusion.6, f32[4,256,256]{2,1,0:T(8,128)} %convolution_multiply_fusion.1), custom_call_target="tpu_custom_call" | custom-call | tf_op online-softmax
  194.0 2.8 fusion.49
  196.9 2.4 convolution_subtract_fusion
  199.2 10.1 %fusion.82 = (f32[4,4096]{1,0:T(4,128)S(1)}, f32[4,4096,256]{1,2,0:T(8,128)}) fusion(bf16[4096,4,64]{0,2,1:T(8,128)(2,1)} %bitcast.89, bf16[256,4,64]{0,2,1:T(8,128)(2,1)S(1)} %copy.60), kind=kOutput, calls=%fused_computation.91 | convolution fusion | flops 549454080 | bytes 19070976 | tf_op jit(solution)/shard_map/sub | solution.py:45
  209.3 2.1 convolution_multiply_fusion
  211.5 4.2 %all-reduce.2.cloned.1.call-done = bf16[66560]{0:T(1024)(128)(2,1)} async-done(((bf16[66560]{0:T(1024)(128)(2,1)}), bf16[66560]{0:T(1024)(128)(2,1)}) %all-reduce.2.cloned.1.call-update) | async-done | bytes 133136 | tf_op jit(solution)/shard_map/psum | solution.py:39
  215.7 0.9 slice_convert_fusion
  217.5 2.5 convolution_convert_fusion.1
  219.9 7.4 %fusion.19 = bf16[4,64,4096]{2,1,0:T(8,128)(2,1)S(1)} fusion(bf16[4,256,64]{1,2,0:T(8,128)(2,1)S(1)} %convolution_convert_fusion.1, f32[4,4096,256]{1,2,0:T(8,128)} %get-tuple-element.21, f32[4,4096]{1,0:T(4,128)S(1)} %get-tuple-element.20), kind=kOutput, calls=%fused_computation.18 | convolution fusion | flops 546308096 | bytes 19070976 | tf_op jit(solution)/shard_map/cye,cea->yca/dot_general | solution.py:136
  227.4 5.6 %convolution_convert_fusion = bf16[4096,1024]{1,0:T(8,128)(2,1)} fusion(bf16[4096,256]{0,1:T(8,128)(2,1)S(1)} %bitcast.88, bf16[256,1024]{1,0:T(8,128)(2,1)S(1)} %copy-done.8), kind=kOutput, calls=%fused_computation.15 | convolution fusion | flops 2151677952 | bytes 11010048 | tf_op jit(solution)/shard_map/dot_general | solution.py:142
  233.0 78.8 %reduce-scatter.2.cloned.1.call-done = bf16[4096,256]{1,0:T(8,128)(2,1)} async-done(((bf16[4096,1024]{1,0:T(8,128)(2,1)}), bf16[4096,256]{1,0:T(8,128)(2,1)}) %reduce-scatter.2.cloned.1.call-update) | async-done | bytes 2097168 | tf_op jit(solution)/shard_map/reduce_scatter | solution.py:143
  (49 shorter events, 4.6 us)
Async XLA Ops:
  6.5 1.4 copy-start
  6.5 209.1 %all-reduce.2.cloned.1.call-start = ((), (), s32[]{:S(2)}) async-start(), calls=%async_computation.1 | async-start | bytes 266240 | tf_op jit(solution)/shard_map/psum | solution.py:39
  120.7 191.2 %reduce-scatter.2.cloned.1.call-start = ((), (), s32[]{:S(2)}) async-start(), calls=%async_computation.2 | async-start | bytes 10485760 | tf_op jit(solution)/shard_map/reduce_scatter | solution.py:143
  125.3 12.4 %copy-start.7 = (f32[4,256,256]{1,2,0:T(8,128)S(1)}, f32[4,256,256]{1,2,0:T(8,128)}, u32[]{:S(2)}) copy-start(f32[4,256,256]{1,2,0:T(8,128)} %bitcast_divide_fusion) | copy-start | bytes 3145732
  140.7 9.9 %copy-start.3 = (f32[4,256,256]{2,1,0:T(8,128)S(1)}, f32[4,256,256]{2,1,0:T(8,128)}, u32[]{:S(2)}) copy-start(f32[4,256,256]{2,1,0:T(8,128)} %convolution_multiply_fusion.5) | copy-start | bytes 3145732
  152.7 10.1 %copy-start.4 = (f32[4,256,256]{2,1,0:T(8,128)S(1)}, f32[4,256,256]{2,1,0:T(8,128)}, u32[]{:S(2)}) copy-start(f32[4,256,256]{2,1,0:T(8,128)} %convolution_multiply_fusion.4) | copy-start | bytes 3145732
  165.0 9.9 %copy-start.5 = (f32[4,256,256]{2,1,0:T(8,128)S(1)}, f32[4,256,256]{2,1,0:T(8,128)}, u32[]{:S(2)}) copy-start(f32[4,256,256]{2,1,0:T(8,128)} %convolution_multiply_fusion.3) | copy-start | bytes 3145732
  177.1 9.9 %copy-start.6 = (f32[4,256,256]{2,1,0:T(8,128)S(1)}, f32[4,256,256]{2,1,0:T(8,128)}, u32[]{:S(2)}) copy-start(f32[4,256,256]{2,1,0:T(8,128)} %convolution_multiply_fusion.2) | copy-start | bytes 3145732
  199.2 10.1 %copy-start.2 = (f32[4,256,256]{2,1,0:T(8,128)S(1)}, f32[4,256,256]{2,1,0:T(8,128)}, u32[]{:S(2)}) copy-start(f32[4,256,256]{2,1,0:T(8,128)} %convolution_multiply_fusion.1) | copy-start | bytes 3145732
  219.9 7.5 %copy-start.8 = (bf16[256,1024]{1,0:T(8,128)(2,1)S(1)}, bf16[256,1024]{1,0:T(8,128)(2,1)}, u32[]{:S(2)}) copy-start(bf16[256,1024]{1,0:T(8,128)(2,1)} %param.5) | copy-start | bytes 1572868
  227.4 84.5 %copy-start.1 = (bf16[3,1024,256]{2,1,0:T(8,128)(2,1)S(1)}, bf16[3,1024,256]{2,1,0:T(8,128)(2,1)}, u32[]{:S(2)}) copy-start(bf16[3,1024,256]{2,1,0:T(8,128)(2,1)} %param.4) | copy-start | bytes 4718596
Sparse Core Ops, SparseCore 0:
  120.8 94.8 all-reduce.1
  233.2 78.6 reduce-scatter.1
where the time goes:
time: 323 us; the launch traced here: 319 us
  matrix products  102 us (32%)
  waiting for transfers between devices  83.1 us (26%)
  blocking collectives  48.9 us (15%)
  Pallas kernels  28.7 us (9%)
  other arithmetic  22.5 us (7%)
  local copies, waits for them, and re-layouts  19.3 us (6%)
  between operations  14.2 us (4%)
    reduce_scatter x1, waiting for transfers between devices, on_device(): lax.psum_scatter(partial_out.astype(jnp.bfloat16), 'tp', scatter_dimensio...  78.8 us
    unnamed x6, Pallas kernels  28.7 us
    all_gather x1, blocking collectives, gather_together(): lines, at, finished = (lax.all_gather(flat, axis), 0, [])  28 us
    pmax x3, blocking collectives, one_axis_at_a_time(): return functools.reduce(lax.pmax, axes, shard)  21 us
    dot_general x6, matrix products, newton_inverse(): jnp.einsum('hij,hjk->hik', prod_az, 7.0 * eye - prod_az, precision=hi)  16.5 us
    unnamed x23, local copies, waits for them, and re-layouts  15.2 us
    dot_general x6, matrix products, newton_inverse(): jnp.einsum('hij,hjk->hik', prod_az, 15.0 * eye - inner, precision=hi)  14.3 us
    dot_general x6, matrix products, newton_inverse(): jnp.einsum('hij,hjk->hik', approx, 13.0 * eye - outer, precision=hi)  13.7 us
  transfers between devices with their start and end apart: 2, of which 2 were waited for; matrix products, arithmetic and copies ran while one was open for 19% of the time, Pallas kernels for 9%

commit v1 on v0

v1 whole, which is shorter than its diff:
```python
import functools
import math

import jax
import jax.numpy as jnp
from jax import lax
from jax.experimental import pallas as pl
from jax.experimental.pallas import tpu as pltpu
from jax.sharding import PartitionSpec as P

HEAD_DIM = 64
MARKS = 256
NEWTON = 6
D = 1024
W = 256
T = 4096
SEG = 512
C = 1024
LOG_SCALE = HEAD_DIM**-0.5 * math.log2(math.e)
bf16, f32 = jnp.bfloat16, jnp.float32
NT = (((1,), (1,)), ((), ()))
MESH = pl.DeviceIdType.MESH


def dot(a, b):
    return jnp.dot(a, b, preferred_element_type=f32)


def dot_nt(a, b):
    return lax.dot_general(a, b, NT, preferred_element_type=f32)


def halves(a):
    hi = a.astype(bf16)
    return hi, (a - hi.astype(f32)).astype(bf16)


def dot3(a, b):
    ah, al = halves(a)
    bh, bl = halves(b)
    return dot(jnp.concatenate([ah, al, ah], 1), jnp.concatenate([bh, bh, bl], 0))


def low_lanes(rows):
    return lax.broadcasted_iota(jnp.int32, (rows, 128), 1) < 64


def one_head(block, head):
    low = low_lanes(block.shape[0])
    return jnp.where(low if head % 2 == 0 else ~low, block, 0.0)


def pair_columns(array, pair):
    return array[:, pair * 128 : (pair + 1) * 128]


def softmax_terms(logits):
    return jnp.exp2(logits - jnp.max(logits, axis=1, keepdims=True))


def kernel(
    n_seq, n_tp,
    x_hbm, w_hbm, wo_hbm, out_hbm,
    x, wk, wv, wq, wo, q, k, v, means, mk_s, mk_r, qm, km, kmt,
    acc, mx, lv_s, lv_r, a_ref, z_ref, mid_s, mid_r, midt, midb, e_own, att, outv,
    load_sem, x_sem, out_sem,
    mk_ss, mk_rs, lv_ss, lv_rs, mid_ss, mid_rs,
    wq_ss, wq_rs, wo_ss, wo_rs, km_ss, km_rs, mt_ss, mt_rs,
):
    seq, tp = lax.axis_index("seq"), lax.axis_index("tp")
    n_chunks = T // C

    def rows_of(i):
        return pl.ds(pl.multiple_of(i * C, C), C)

    loads = [
        pltpu.make_async_copy(w_hbm.at[1], wk, load_sem.at[0]),
        pltpu.make_async_copy(w_hbm.at[0], wq.at[tp], load_sem.at[1]),
        pltpu.make_async_copy(w_hbm.at[2], wv, load_sem.at[2]),
        pltpu.make_async_copy(
            wo_hbm.at[:, pl.ds(pl.multiple_of(tp * W, W), W)], wo.at[tp], load_sem.at[3]
        ),
    ]

    def x_load(i):
        return pltpu.make_async_copy(x_hbm.at[rows_of(i)], x.at[rows_of(i)], x_sem.at[i])

    loads[0].start()
    loads[1].start()
    for i in range(n_chunks):
        x_load(i).start()
    loads[2].start()
    loads[3].start()

    barrier = pltpu.get_barrier_semaphore()

    @pl.loop(1, n_seq)
    def _(j):
        pl.semaphore_signal(
            barrier, inc=1, device_id={"seq": lax.rem(seq + j, n_seq)}, device_id_type=MESH
        )

    for j in range(1, n_tp):
        pl.semaphore_signal(
            barrier, inc=1, device_id={"tp": lax.rem(tp + j, n_tp)}, device_id_type=MESH
        )
    pl.semaphore_wait(barrier, n_seq - 1 + n_tp - 1)

    def to_tp(j):
        return lax.rem(tp + j, n_tp)

    def from_tp(j):
        return lax.rem(tp + n_tp - j, n_tp)

    def remote_tp(src, dst_of, ss, rs, j):
        return pltpu.make_async_remote_copy(
            src_ref=src, dst_ref=dst_of, send_sem=ss.at[j], recv_sem=rs.at[j],
            device_id={"tp": to_tp(j)}, device_id_type=MESH,
        )

    def wq_copy(j, slot):
        return remote_tp(w_hbm.at[0], wq.at[slot], wq_ss, wq_rs, j)

    def wo_copy(j, slot):
        columns = pl.ds(pl.multiple_of(to_tp(j) * W, W), W)
        return remote_tp(wo_hbm.at[:, columns], wo.at[slot], wo_ss, wo_rs, j)

    def km_copy(j, slot):
        return remote_tp(kmt.at[tp], kmt.at[slot], km_ss, km_rs, j)

    def mt_copy(j, slot):
        return remote_tp(midt.at[tp], midt.at[slot], mt_ss, mt_rs, j)

    for j in range(1, n_tp):
        wq_copy(j, tp).start()
    for j in range(1, n_tp):
        wo_copy(j, tp).start()

    loads[0].wait()
    loads[1].wait()

    @pl.loop(0, n_chunks)
    def _(i):
        x_load(i).wait()
        rows = rows_of(i)
        xc = x[rows, :]
        kp = dot(xc, wk[...])
        qp = dot(xc, wq[tp]) * LOG_SCALE
        k[rows, :] = kp.astype(bf16)
        q[tp, rows, :] = qp.astype(bf16)
        for s in range(C // SEG):
            at = i * (C // SEG) + s
            part = slice(s * SEG, (s + 1) * SEG)
            means[pl.ds(at, 1), :] = jnp.sum(qp[part], axis=0, keepdims=True) * (1.0 / SEG)
            means[pl.ds(8 + at, 1), :] = jnp.sum(kp[part], axis=0, keepdims=True) * (1.0 / SEG)

    def exchange(copy_of, slots):
        @pl.loop(1, n_seq)
        def _(j):
            copy_of(j, seq).start()

    def finish(copy_of):
        @pl.loop(1, n_seq)
        def _(j):
            copy_of(j, lax.rem(seq + n_seq - j, n_seq)).wait_recv()

    def finish_sends(copy_of):
        @pl.loop(1, n_seq)
        def _(j):
            copy_of(j, seq).wait_send()

    def remote_seq(src, dst, ss, rs, j):
        return pltpu.make_async_remote_copy(
            src_ref=src, dst_ref=dst, send_sem=ss.at[j], recv_sem=rs.at[j],
            device_id={"seq": lax.rem(seq + j, n_seq)}, device_id_type=MESH,
        )

    def mk_copy(j, slot):
        return remote_seq(mk_s, mk_r.at[slot], mk_ss, mk_rs, j)

    def lv_copy(j, slot):
        return remote_seq(lv_s.at[lax.rem(seq + j, n_seq)], lv_r.at[slot], lv_ss, lv_rs, j)

    def mid_copy(j, slot):
        return remote_seq(mid_s, mid_r.at[slot], mid_ss, mid_rs, j)

    mk_s[...] = means[...].astype(bf16)
    exchange(mk_copy, mk_r)
    mk_r[seq] = means[...].astype(bf16)

    loads[2].wait()
    ones = jnp.ones((C, 128), bf16)

    @pl.loop(0, n_chunks)
    def _(i):
        rows = rows_of(i)
        vp = dot(x[rows, :], wv[...]).astype(bf16)
        for p in range(2):
            v[p, rows, 0:128] = pair_columns(vp, p)
            v[p, rows, 128:256] = ones

    finish(mk_copy)
    marks = mk_r[...].astype(f32)
    q_marks = marks[:, 0:8, :].reshape(MARKS, W)
    k_marks = marks[:, 8:16, :].reshape(MARKS, W)
    kmt[tp] = k_marks.astype(bf16)
    for j in range(1, n_tp):
        km_copy(j, tp).start()
    for h in range(4):
        qm[h] = one_head(pair_columns(q_marks, h // 2), h).astype(bf16)
        km[tp * 4 + h] = one_head(pair_columns(k_marks, h // 2), h).astype(bf16)

    acc[...] = jnp.zeros_like(acc)
    mx[...] = jnp.full_like(mx, -jnp.inf)

    @pl.loop(0, n_chunks)
    def _(i):
        rows = rows_of(i)
        for h in range(4):
            p = h // 2
            s = dot_nt(qm[h], k[rows, p * 128 : (p + 1) * 128])
            before = mx[h]
            now = jnp.maximum(before, jnp.max(s, axis=1, keepdims=True))
            e = jnp.exp2(s - now[:, :1]).astype(bf16)
            mx[h] = now
            fade = jnp.exp2(before - now)
            acc[h] = acc[h] * jnp.concatenate([fade, fade], 1) + dot(e, v[p, rows, :])

    sub = lax.broadcasted_iota(jnp.int32, (8, W), 0)
    for p in range(2):
        even, odd = acc[2 * p], acc[2 * p + 1]
        mean_values = jnp.where(
            low_lanes(MARKS), even[:, :128] / even[:, 128:], odd[:, :128] / odd[:, 128:]
        ).T
        for i, r in enumerate((even, odd)):
            h = 2 * p + i
            level = (mx[h] + jnp.log2(r[:, 128:])).T[0:8, :]
            first = level.astype(bf16).astype(f32)
            second = (level - first).astype(bf16).astype(f32)
            third = level - first - second
            lines = jnp.where(
                sub == 0, first, jnp.where(sub == 1, second, jnp.where(sub == 2, third, 0.0))
            )
            for b in range(8):
                part = mean_values[i * 64 + b * 8 : i * 64 + b * 8 + 8, :]
                lv_s[h * 8 + b] = jnp.concatenate([part, lines], 0).astype(bf16)
    exchange(lv_copy, lv_r)
    lv_r[seq] = lv_s[seq]

    head = lax.div(seq, 8)
    terms = softmax_terms(dot_nt(qm[head], km[tp * 4 + head]))
    kernel_a = terms / jnp.sum(terms, axis=1, keepdims=True)
    col = jnp.max(jnp.sum(kernel_a, axis=0, keepdims=True), axis=1, keepdims=True)
    row = jnp.max(jnp.sum(kernel_a, axis=1, keepdims=True), axis=0, keepdims=True)
    a_ref[...] = kernel_a
    z_ref[...] = kernel_a.T / (col * row)
    for j in range(1, n_tp):
        wq_copy(j, from_tp(j)).wait_recv()

    units = 3 * (T // 512) // NEWTON

    @pl.loop(0, NEWTON)
    def _(turn):
        def other_queries(i):
            unit = turn * units + i
            t = to_tp(1 + lax.div(unit, 8))
            rows = pl.ds(pl.multiple_of(lax.rem(unit, 8) * 512, 512), 512)
            q[t, rows, :] = (dot(x[rows, :], wq[t]) * LOG_SCALE).astype(bf16)

        eye = jnp.where(
            lax.broadcasted_iota(jnp.int32, (MARKS, MARKS), 0)
            == lax.broadcasted_iota(jnp.int32, (MARKS, MARKS), 1),
            1.0,
            0.0,
        )
        z = z_ref[...]
        az = dot3(a_ref[...], z)
        other_queries(0)
        inner = dot3(az, 7.0 * eye - az)
        other_queries(1)
        outer = dot3(az, 15.0 * eye - inner)
        other_queries(2)
        z_ref[...] = 0.25 * dot3(z, 13.0 * eye - outer)
        other_queries(3)

    finish(lv_copy)
    lv = lv_r[...].astype(f32)
    level = lv[:, 8:9, :] + lv[:, 9:10, :] + lv[:, 10:11, :]
    share = jnp.exp2(level - jnp.max(level, axis=0, keepdims=True))
    columns = jnp.sum(lv[:, 0:8, :] * share, axis=0) / jnp.sum(share, axis=0)
    ch, cl = halves(columns)
    zh, zl = halves(z_ref[...])
    middle = dot_nt(jnp.concatenate([ch, cl, ch], 1), jnp.concatenate([zh, zh, zl], 1))
    mid_s[...] = middle
    exchange(mid_copy, mid_r)
    mid_r[seq] = middle

    @pl.loop(0, n_chunks)
    def _(i):
        rows = rows_of(i)
        for h in range(4):
            p = h // 2
            logits = dot_nt(q[tp, rows, p * 128 : (p + 1) * 128], km[tp * 4 + h])
            e_own[rows, h * MARKS : (h + 1) * MARKS] = softmax_terms(logits).astype(bf16)

    def place_middle(t):
        m = midt[t].astype(f32)
        low = low_lanes(MARKS)
        for p in range(2):
            both = pair_columns(m, p)
            for i in range(2):
                mask = low if i == 0 else ~low
                midb[t * 2 + p, i * MARKS : (i + 1) * MARKS, :] = jnp.concatenate(
                    [jnp.where(mask, both, 0.0), jnp.where(mask, 1.0, 0.0)], 1
                ).astype(bf16)

    finish(mid_copy)
    midt[tp] = mid_r[...].reshape(W, MARKS).T.astype(bf16)
    for j in range(1, n_tp):
        mt_copy(j, tp).start()
    place_middle(tp)

    def normalised(r):
        return (r[:, :128] * (1.0 / r[:, 128:])).astype(bf16)

    @pl.loop(0, n_chunks)
    def _(i):
        rows = rows_of(i)
        for p in range(2):
            r = dot(e_own[rows, p * 512 : (p + 1) * 512], midb[tp * 2 + p])
            att[rows, p * 128 : (p + 1) * 128] = normalised(r)

    loads[3].wait()
    for j in range(1, n_tp):
        t = from_tp(j)
        km_copy(j, t).wait_recv()
        others = kmt[t].astype(f32)
        for h in range(4):
            km[t * 4 + h] = one_head(pair_columns(others, h // 2), h).astype(bf16)
        wo_copy(j, t).wait_recv()
    for j in range(1, n_tp):
        t = from_tp(j)
        mt_copy(j, t).wait_recv()
        place_middle(t)

    def out_copy(i):
        return pltpu.make_async_copy(outv.at[rows_of(i)], out_hbm.at[rows_of(i)], out_sem.at[i])

    @pl.loop(0, n_chunks)
    def _(i):
        rows = rows_of(i)
        total = dot(att[rows, :], wo[tp])
        for j in range(1, n_tp):
            t = to_tp(j)
            parts = []
            for p in range(2):
                qc = q[t, rows, p * 128 : (p + 1) * 128]
                e = [
                    softmax_terms(dot_nt(qc, km[t * 4 + 2 * p + b])).astype(bf16) for b in range(2)
                ]
                parts.append(normalised(dot(jnp.concatenate(e, 1), midb[t * 2 + p])))
            total = total + dot(jnp.concatenate(parts, 1), wo[t])
        outv[rows, :] = total.astype(bf16)
        out_copy(i).start()

    for copy_of in (mk_copy, lv_copy, mid_copy):
        finish_sends(copy_of)
    for copy_of in (wq_copy, wo_copy, km_copy, mt_copy):
        for j in range(1, n_tp):
            copy_of(j, tp).wait_send()
    for i in range(n_chunks):
        out_copy(i).wait()


def on_device(n_seq, n_tp, tokens, w_qkv, w_out):
    vmem = pltpu.VMEM
    sems = pltpu.SemaphoreType.DMA
    scratch = [
        vmem((T, D), bf16),
        vmem((D, W), bf16),
        vmem((D, W), bf16),
        vmem((n_tp, D, W), bf16),
        vmem((n_tp, W, W), bf16),
        vmem((n_tp, T, W), bf16),
        vmem((T, W), bf16),
        vmem((2, T, 256), bf16),
        vmem((16, W), f32),
        vmem((16, W), bf16),
        vmem((n_seq, 16, W), bf16),
        vmem((4, MARKS, 128), bf16),
        vmem((4 * n_tp, MARKS, 128), bf16),
        vmem((n_tp, MARKS, W), bf16),
        vmem((4, MARKS, 256), f32),
        vmem((4, MARKS, 128), f32),
        vmem((n_seq, 16, MARKS), bf16),
        vmem((n_seq, 16, MARKS), bf16),
        vmem((MARKS, MARKS), f32),
        vmem((MARKS, MARKS), f32),
        vmem((8, MARKS), f32),
        vmem((n_seq, 8, MARKS), f32),
        vmem((n_tp, MARKS, W), bf16),
        vmem((2 * n_tp, 2 * MARKS, 256), bf16),
        vmem((T, 4 * MARKS), bf16),
        vmem((T, W), bf16),
        vmem((T, W), bf16),
        sems((4,)), sems((T // C,)), sems((T // C,)),
        *[sems((n_seq,))] * 6,
        *[sems((n_tp,))] * 8,
    ]
    hbm = pl.BlockSpec(memory_space=pl.ANY)
    return pl.pallas_call(
        functools.partial(kernel, n_seq, n_tp),
        out_shape=jax.ShapeDtypeStruct((T, W), bf16),
        in_specs=[hbm] * 3,
        out_specs=hbm,
        scratch_shapes=scratch,
        compiler_params=pltpu.CompilerParams(
            collective_id=0, has_side_effects=True, vmem_limit_bytes=60 * 2**20
        ),
    )(tokens, w_qkv, w_out)


def solution(mesh):
    return jax.shard_map(
        functools.partial(on_device, mesh.shape["seq"], mesh.shape["tp"]),
        mesh=mesh,
        in_specs=(P("seq", None), P(None, None, "tp"), P("tp", None)),
        out_specs=P("seq", "tp"),
        check_vma=False,
    )
```

time: 323 us -> 86.2 us (0.27); the launches traced: 319 us -> 86 us
  matrix products: 102 us -> 0 us
  waiting for transfers between devices: 83.1 us -> 0 us
  Pallas kernels: 28.7 us -> 83 us
  blocking collectives: 48.9 us -> 0 us
  other arithmetic: 22.5 us -> 0 us
  local copies, waits for them, and re-layouts: 19.3 us -> 3.05 us
  between operations: 14.2 us -> 0.01 us
    dot_general x25 -> x0, matrix products: 91.4 us -> none  [the longest x6 16.5 us: newton_inverse(): jnp.einsum('hij,hjk->hik', prod_az, 7.0 * eye - prod_az, precision=hi)]
    pallas_call x0 -> x1, Pallas kernels: none -> 83 us  [on_device(): pl.pallas_call(functools.partial(kernel, n_seq, n_tp), out_shape=jax.Shap...]
    reduce_scatter x1 -> x0, waiting for transfers between devices: 78.8 us -> none  [on_device(): lax.psum_scatter(partial_out.astype(jnp.bfloat16), 'tp', scatter_dimensio...]
    unnamed x6 -> x0, Pallas kernels: 28.7 us -> none
    all_gather x1 -> x0, blocking collectives: 28 us -> none  [gather_together(): lines, at, finished = (lax.all_gather(flat, axis), 0, [])]
    pmax x3 -> x0, blocking collectives: 21 us -> none  [one_axis_at_a_time(): return functools.reduce(lax.pmax, axes, shard)]
    reduce_sum x4 -> x0, other arithmetic: 14.1 us -> none  [the longest x1 8.62 us: on_device(): block_total = jnp.sum(exponent_terms, axis=-1)]
    unnamed x23 -> x1, local copies, waits for them, and re-layouts: 15.2 us -> 3.05 us
  transfers between devices with their start and end apart: 2 -> 0, of which waited for: 2 -> 0; matrix products, arithmetic and copies ran while one was open for 19% -> 0% of each run, Pallas kernels for 9% -> 0%
where the time goes in v1:
time: 86.2 us; the launch traced here: 86 us
  Pallas kernels  83 us (96%)
  local copies, waits for them, and re-layouts  3.05 us (4%)
    pallas_call x1, Pallas kernels, on_device(): pl.pallas_call(functools.partial(kernel, n_seq, n_tp), out_shape=jax.Shap...  83 us
    unnamed x1, local copies, waits for them, and re-layouts  3.05 us

profile of v1, /device:TPU:1, one launch (start us, length us, event | category | flops | bytes accessed | tf_op | source)
XLA Modules:
  0.0 86.0 jit_solution(17410363496352110075)
XLA Ops:
  0.0 83.0 %shard_map.37 = bf16[4096,256]{1,0:T(8,128)(2,1)} custom-call(bf16[4096,1024]{1,0:T(8,128)(2,1)} %x_hbm.1, bf16[3,1024,256]{2,1,0:T(8,128)(2,1)} %w_hbm.1, bf16[256,1024]{1,0:T(8,128)(2,1)} %wo_hbm.1), custom_call_target="tpu_custom_call" | custom-call | tf_op jit(solution)/shard_map/pallas_call | solution.py:411
  83.0 3.0 %copy.5 = bf16[4096,256]{1,0:T(8,128)(2,1)} copy(bf16[4096,256]{1,0:T(8,128)(2,1)} %shard_map.37) | data formatting | bytes 4194304

commit v2 on v1

--- a/solution.py
+++ b/solution.py
@@ -20,6 +20,7 @@
 bf16, f32 = jnp.bfloat16, jnp.float32
 NT = (((1,), (1,)), ((), ()))
 MESH = pl.DeviceIdType.MESH
+ORDER = (3, 1, 2)
 
 
 def dot(a, b):
@@ -62,16 +63,25 @@
     n_seq, n_tp,
     x_hbm, w_hbm, wo_hbm, out_hbm,
     x, wk, wv, wq, wo, q, k, v, means, mk_s, mk_r, qm, km, kmt,
-    acc, mx, lv_s, lv_r, a_ref, z_ref, mid_s, mid_r, midt, midb, e_own, att, outv,
+    acc, mx, lv_s, lv_r, a_ref, z_ref, mid_s, mid_r, midt, midb, e_a, e_b, outv,
     load_sem, x_sem, out_sem,
     mk_ss, mk_rs, lv_ss, lv_rs, mid_ss, mid_rs,
-    wq_ss, wq_rs, wo_ss, wo_rs, km_ss, km_rs, mt_ss, mt_rs,
+    wq_sems, wo_sems, km_sems, mt_sems,
 ):
     seq, tp = lax.axis_index("seq"), lax.axis_index("tp")
+    core = lax.rem(seq, 2)
     n_chunks = T // C
 
     def rows_of(i):
         return pl.ds(pl.multiple_of(i * C, C), C)
+
+    def to_tp(j):
+        return lax.rem(tp + j, n_tp)
+
+    def from_tp(j):
+        return lax.rem(tp + n_tp - j, n_tp)
+
+    barrier = pltpu.get_barrier_semaphore()
 
     loads = [
         pltpu.make_async_copy(w_hbm.at[1], wk, load_sem.at[0]),
@@ -92,8 +102,6 @@
     loads[2].start()
     loads[3].start()
 
-    barrier = pltpu.get_barrier_semaphore()
-
     @pl.loop(1, n_seq)
     def _(j):
         pl.semaphore_signal(
@@ -102,45 +110,56 @@
 
     for j in range(1, n_tp):
         pl.semaphore_signal(
-            barrier, inc=1, device_id={"tp": lax.rem(tp + j, n_tp)}, device_id_type=MESH
+            barrier, inc=1, device_id={"tp": to_tp(j)}, device_id_type=MESH
         )
-    pl.semaphore_wait(barrier, n_seq - 1 + n_tp - 1)
-
-    def to_tp(j):
-        return lax.rem(tp + j, n_tp)
-
-    def from_tp(j):
-        return lax.rem(tp + n_tp - j, n_tp)
-
-    def remote_tp(src, dst_of, ss, rs, j):
-        return pltpu.make_async_remote_copy(
-            src_ref=src, dst_ref=dst_of, send_sem=ss.at[j], recv_sem=rs.at[j],
-            device_id={"tp": to_tp(j)}, device_id_type=MESH,
-        )
-
-    def wq_copy(j, slot):
-        return remote_tp(w_hbm.at[0], wq.at[slot], wq_ss, wq_rs, j)
-
-    def wo_copy(j, slot):
-        columns = pl.ds(pl.multiple_of(to_tp(j) * W, W), W)
-        return remote_tp(wo_hbm.at[:, columns], wo.at[slot], wo_ss, wo_rs, j)
-
-    def km_copy(j, slot):
-        return remote_tp(kmt.at[tp], kmt.at[slot], km_ss, km_rs, j)
-
-    def mt_copy(j, slot):
-        return remote_tp(midt.at[tp], midt.at[slot], mt_ss, mt_rs, j)
-
-    for j in range(1, n_tp):
-        wq_copy(j, tp).start()
-    for j in range(1, n_tp):
-        wo_copy(j, tp).start()
-
-    loads[0].wait()
-    loads[1].wait()
-
-    @pl.loop(0, n_chunks)
-    def _(i):
+
+    class Gather:
+        def __init__(self, source, ref, sems):
+            half = ref.shape[1] // 2
+            self.source, self.ref, self.sems = source, ref, sems
+            self.mine = pl.ds(pl.multiple_of(core * half, half), half)
+            self.other = pl.ds(pl.multiple_of((1 - core) * half, half), half)
+
+        def over(self, j, slot):
+            return pltpu.make_async_remote_copy(
+                src_ref=self.source(j, self.mine), dst_ref=self.ref.at[slot, self.mine],
+                send_sem=self.sems.at[0, j], recv_sem=self.sems.at[1, j],
+                device_id={"tp": to_tp(j)}, device_id_type=MESH,
+            )
+
+        def across(self, j, part):
+            t = from_tp(j)
+            return pltpu.make_async_remote_copy(
+                src_ref=self.ref.at[t, part], dst_ref=self.ref.at[t, part],
+                send_sem=self.sems.at[2, j], recv_sem=self.sems.at[3, j],
+                device_id={"seq": seq + 1 - 2 * core}, device_id_type=MESH,
+            )
+
+        def send(self):
+            for j in ORDER:
+                self.over(j, tp).start()
+
+        def swap(self, j):
+            self.over(j, from_tp(j)).wait_recv()
+            self.across(j, self.mine).start()
+
+        def ready(self, j):
+            self.across(j, self.other).wait_recv()
+
+        def drain(self):
+            for j in ORDER:
+                self.over(j, tp).wait_send()
+                self.across(j, self.mine).wait_send()
+
+    def columns_of(j):
+        return pl.ds(pl.multiple_of(to_tp(j) * W, W), W)
+
+    wq_all = Gather(lambda j, part: w_hbm.at[0, part], wq, wq_sems)
+    wo_all = Gather(lambda j, part: wo_hbm.at[part, columns_of(j)], wo, wo_sems)
+    km_all = Gather(lambda j, part: kmt.at[tp, part], kmt, km_sems)
+    mt_all = Gather(lambda j, part: midt.at[tp, part], midt, mt_sems)
+
+    def own_rows(i):
         x_load(i).wait()
         rows = rows_of(i)
         xc = x[rows, :]
@@ -154,7 +173,18 @@
             means[pl.ds(at, 1), :] = jnp.sum(qp[part], axis=0, keepdims=True) * (1.0 / SEG)
             means[pl.ds(8 + at, 1), :] = jnp.sum(kp[part], axis=0, keepdims=True) * (1.0 / SEG)
 
-    def exchange(copy_of, slots):
+    loads[0].wait()
+    loads[1].wait()
+    own_rows(0)
+    pl.semaphore_wait(barrier, n_seq - 1 + n_tp - 1)
+    wq_all.send()
+    wo_all.send()
+
+    @pl.loop(1, n_chunks)
+    def _(i):
+        own_rows(i)
+
+    def exchange(copy_of):
         @pl.loop(1, n_seq)
         def _(j):
             copy_of(j, seq).start()
@@ -185,27 +215,37 @@
         return remote_seq(mid_s, mid_r.at[slot], mid_ss, mid_rs, j)
 
     mk_s[...] = means[...].astype(bf16)
-    exchange(mk_copy, mk_r)
+    exchange(mk_copy)
     mk_r[seq] = means[...].astype(bf16)
 
     loads[2].wait()
     ones = jnp.ones((C, 128), bf16)
 
-    @pl.loop(0, n_chunks)
-    def _(i):
+    def own_values(i):
         rows = rows_of(i)
         vp = dot(x[rows, :], wv[...]).astype(bf16)
         for p in range(2):
             v[p, rows, 0:128] = pair_columns(vp, p)
             v[p, rows, 128:256] = ones
 
+    def other_queries(t, rows):
+        q[t, rows, :] = (dot(x[rows, :], wq[t]) * LOG_SCALE).astype(bf16)
+
+    pl.loop(0, n_chunks - 1)(own_values)
+    wq_all.swap(ORDER[0])
+    own_values(n_chunks - 1)
+    wq_all.ready(ORDER[0])
+
+    @pl.loop(0, n_chunks)
+    def _(i):
+        other_queries(from_tp(ORDER[0]), rows_of(i))
+
     finish(mk_copy)
     marks = mk_r[...].astype(f32)
     q_marks = marks[:, 0:8, :].reshape(MARKS, W)
     k_marks = marks[:, 8:16, :].reshape(MARKS, W)
     kmt[tp] = k_marks.astype(bf16)
-    for j in range(1, n_tp):
-        km_copy(j, tp).start()
+    km_all.send()
     for h in range(4):
         qm[h] = one_head(pair_columns(q_marks, h // 2), h).astype(bf16)
         km[tp * 4 + h] = one_head(pair_columns(k_marks, h // 2), h).astype(bf16)
@@ -226,6 +266,8 @@
             fade = jnp.exp2(before - now)
             acc[h] = acc[h] * jnp.concatenate([fade, fade], 1) + dot(e, v[p, rows, :])
 
+    for j in ORDER[1:]:
+        wq_all.swap(j)
     sub = lax.broadcasted_iota(jnp.int32, (8, W), 0)
     for p in range(2):
         even, odd = acc[2 * p], acc[2 * p + 1]
@@ -244,8 +286,12 @@
             for b in range(8):
                 part = mean_values[i * 64 + b * 8 : i * 64 + b * 8 + 8, :]
                 lv_s[h * 8 + b] = jnp.concatenate([part, lines], 0).astype(bf16)
-    exchange(lv_copy, lv_r)
+    exchange(lv_copy)
     lv_r[seq] = lv_s[seq]
+    for j in ORDER:
+        km_all.swap(j)
+    for j in ORDER:
+        wo_all.swap(j)
 
     head = lax.div(seq, 8)
     terms = softmax_terms(dot_nt(qm[head], km[tp * 4 + head]))
@@ -254,19 +300,15 @@
     row = jnp.max(jnp.sum(kernel_a, axis=1, keepdims=True), axis=0, keepdims=True)
     a_ref[...] = kernel_a
     z_ref[...] = kernel_a.T / (col * row)
-    for j in range(1, n_tp):
-        wq_copy(j, from_tp(j)).wait_recv()
-
-    units = 3 * (T // 512) // NEWTON
+    for j in ORDER[1:]:
+        wq_all.ready(j)
+
+    def unit(u):
+        t = lax.rem(tp + 3 + 3 * lax.div(u, 16), n_tp)
+        other_queries(t, pl.ds(pl.multiple_of(lax.rem(u, 16) * 256, 256), 256))
 
     @pl.loop(0, NEWTON)
     def _(turn):
-        def other_queries(i):
-            unit = turn * units + i
-            t = to_tp(1 + lax.div(unit, 8))
-            rows = pl.ds(pl.multiple_of(lax.rem(unit, 8) * 512, 512), 512)
-            q[t, rows, :] = (dot(x[rows, :], wq[t]) * LOG_SCALE).astype(bf16)
-
         eye = jnp.where(
             lax.broadcasted_iota(jnp.int32, (MARKS, MARKS), 0)
             == lax.broadcasted_iota(jnp.int32, (MARKS, MARKS), 1),
@@ -275,13 +317,13 @@
         )
         z = z_ref[...]
         az = dot3(a_ref[...], z)
-        other_queries(0)
+        unit(turn * 4)
         inner = dot3(az, 7.0 * eye - az)
-        other_queries(1)
+        unit(turn * 4 + 1)
         outer = dot3(az, 15.0 * eye - inner)
-        other_queries(2)
+        unit(turn * 4 + 2)
         z_ref[...] = 0.25 * dot3(z, 13.0 * eye - outer)
-        other_queries(3)
+        unit(turn * 4 + 3)
 
     finish(lv_copy)
     lv = lv_r[...].astype(f32)
@@ -292,16 +334,25 @@
     zh, zl = halves(z_ref[...])
     middle = dot_nt(jnp.concatenate([ch, cl, ch], 1), jnp.concatenate([zh, zh, zl], 1))
     mid_s[...] = middle
-    exchange(mid_copy, mid_r)
+    exchange(mid_copy)
     mid_r[seq] = middle
+
+    def terms_of(t, e, rows):
+        for h in range(4):
+            p = h // 2
+            logits = dot_nt(q[t, rows, p * 128 : (p + 1) * 128], km[t * 4 + h])
+            e[rows, h * MARKS : (h + 1) * MARKS] = softmax_terms(logits).astype(bf16)
+
+    def attended_of(t, e, rows):
+        for p in range(2):
+            r = dot(e[rows, p * 512 : (p + 1) * 512], midb[t * 2 + p])
+            q[t, rows, p * 128 : (p + 1) * 128] = (r[:, :128] * (1.0 / r[:, 128:])).astype(bf16)
+
+    pl.loop(24, 32)(unit)
 
     @pl.loop(0, n_chunks)
     def _(i):
-        rows = rows_of(i)
-        for h in range(4):
-            p = h // 2
-            logits = dot_nt(q[tp, rows, p * 128 : (p + 1) * 128], km[tp * 4 + h])
-            e_own[rows, h * MARKS : (h + 1) * MARKS] = softmax_terms(logits).astype(bf16)
+        terms_of(tp, e_a, rows_of(i))
 
     def place_middle(t):
         m = midt[t].astype(f32)
@@ -316,58 +367,52 @@
 
     finish(mid_copy)
     midt[tp] = mid_r[...].reshape(W, MARKS).T.astype(bf16)
-    for j in range(1, n_tp):
-        mt_copy(j, tp).start()
+    mt_all.send()
     place_middle(tp)
-
-    def normalised(r):
-        return (r[:, :128] * (1.0 / r[:, 128:])).astype(bf16)
+    for j in ORDER:
+        t = from_tp(j)
+        km_all.ready(j)
+        others = kmt[t].astype(f32)
+        for h in range(4):
+            km[t * 4 + h] = one_head(pair_columns(others, h // 2), h).astype(bf16)
+        wo_all.ready(j)
+    loads[3].wait()
+
+    groups = [tp] + [from_tp(j) for j in ORDER]
+    buffers = (e_a, e_b)
+
+    def step(g, i):
+        rows = rows_of(i)
+        attended_of(groups[g], buffers[g % 2], rows)
+        terms_of(groups[g + 1], buffers[(g + 1) % 2], rows)
+
+    pl.loop(0, n_chunks - 1)(functools.partial(step, 0))
+    for j in ORDER:
+        mt_all.swap(j)
+    step(0, n_chunks - 1)
+    for j in ORDER:
+        mt_all.ready(j)
+        place_middle(from_tp(j))
+    pl.loop(0, n_chunks)(functools.partial(step, 1))
+    pl.loop(0, n_chunks)(functools.partial(step, 2))
+
+    def out_copy(i):
+        return pltpu.make_async_copy(outv.at[rows_of(i)], out_hbm.at[rows_of(i)], out_sem.at[i])
 
     @pl.loop(0, n_chunks)
     def _(i):
         rows = rows_of(i)
-        for p in range(2):
-            r = dot(e_own[rows, p * 512 : (p + 1) * 512], midb[tp * 2 + p])
-            att[rows, p * 128 : (p + 1) * 128] = normalised(r)
-
-    loads[3].wait()
-    for j in range(1, n_tp):
-        t = from_tp(j)
-        km_copy(j, t).wait_recv()
-        others = kmt[t].astype(f32)
-        for h in range(4):
-            km[t * 4 + h] = one_head(pair_columns(others, h // 2), h).astype(bf16)
-        wo_copy(j, t).wait_recv()
-    for j in range(1, n_tp):
-        t = from_tp(j)
-        mt_copy(j, t).wait_recv()
-        place_middle(t)
-
-    def out_copy(i):
-        return pltpu.make_async_copy(outv.at[rows_of(i)], out_hbm.at[rows_of(i)], out_sem.at[i])
-
-    @pl.loop(0, n_chunks)
-    def _(i):
-        rows = rows_of(i)
-        total = dot(att[rows, :], wo[tp])
-        for j in range(1, n_tp):
-            t = to_tp(j)
-            parts = []
-            for p in range(2):
-                qc = q[t, rows, p * 128 : (p + 1) * 128]
-                e = [
-                    softmax_terms(dot_nt(qc, km[t * 4 + 2 * p + b])).astype(bf16) for b in range(2)
-                ]
-                parts.append(normalised(dot(jnp.concatenate(e, 1), midb[t * 2 + p])))
-            total = total + dot(jnp.concatenate(parts, 1), wo[t])
+        attended_of(groups[3], buffers[1], rows)
+        total = dot(q[groups[0], rows, :], wo[groups[0]])
+        for t in groups[1:]:
+            total = total + dot(q[t, rows, :], wo[t])
         outv[rows, :] = total.astype(bf16)
         out_copy(i).start()
 
     for copy_of in (mk_copy, lv_copy, mid_copy):
         finish_sends(copy_of)
-    for copy_of in (wq_copy, wo_copy, km_copy, mt_copy):
-        for j in range(1, n_tp):
-            copy_of(j, tp).wait_send()
+    for gather in (wq_all, wo_all, km_all, mt_all):
+        gather.drain()
     for i in range(n_chunks):
         out_copy(i).wait()
 
@@ -401,11 +446,11 @@
         vmem((n_tp, MARKS, W), bf16),
         vmem((2 * n_tp, 2 * MARKS, 256), bf16),
         vmem((T, 4 * MARKS), bf16),
-        vmem((T, W), bf16),
+        vmem((T, 4 * MARKS), bf16),
         vmem((T, W), bf16),
         sems((4,)), sems((T // C,)), sems((T // C,)),
         *[sems((n_seq,))] * 6,
-        *[sems((n_tp,))] * 8,
+        *[sems((4, n_tp))] * 4,
     ]
     hbm = pl.BlockSpec(memory_space=pl.ANY)
     return pl.pallas_call(

time: 86.2 us -> 83.5 us (0.969)
  Pallas kernels: 83 us -> 80.3 us
    pallas_call x1, Pallas kernels: 83 us -> 80.3 us  [on_device(): pl.pallas_call(functools.partial(kernel, n_seq, n_tp), out_shape=jax.Shap...]
where the time goes in v2:
time: 83.5 us; the launch traced here: 83.3 us
  Pallas kernels  80.3 us (96%)
  local copies, waits for them, and re-layouts  3.05 us (4%)
    pallas_call x1, Pallas kernels, on_device(): pl.pallas_call(functools.partial(kernel, n_seq, n_tp), out_shape=jax.Shap...  80.3 us
    unnamed x1, local copies, waits for them, and re-layouts  3.05 us

profile of v2, /device:TPU:1, one launch (start us, length us, event | category | flops | bytes accessed | tf_op | source)
XLA Modules:
  0.0 83.3 jit_solution(15986330166548962645)
XLA Ops:
  0.0 80.3 %shard_map.37 = bf16[4096,256]{1,0:T(8,128)(2,1)} custom-call(bf16[4096,1024]{1,0:T(8,128)(2,1)} %x_hbm.1, bf16[3,1024,256]{2,1,0:T(8,128)(2,1)} %w_hbm.1, bf16[256,1024]{1,0:T(8,128)(2,1)} %wo_hbm.1), custom_call_target="tpu_custom_call" | custom-call | tf_op jit(solution)/shard_map/pallas_call | solution.py:456
  80.3 3.0 %copy.5 = bf16[4096,256]{1,0:T(8,128)(2,1)} copy(bf16[4096,256]{1,0:T(8,128)(2,1)} %shard_map.37) | data formatting | bytes 4194304

commit v3 on v2

v3 whole, which is shorter than its diff:
```python
import functools
import math

import jax
import jax.numpy as jnp
from jax import lax
from jax.experimental import pallas as pl
from jax.experimental.pallas import tpu as pltpu
from jax.sharding import PartitionSpec as P

HEAD_DIM = 64
MARKS = 256
NEWTON = 6
UNITS = 7
D = 1024
W = 256
T = 4096
SEG = 512
C = 1024
LOG_SCALE = HEAD_DIM**-0.5 * math.log2(math.e)
bf16, f32 = jnp.bfloat16, jnp.float32
NT = (((1,), (1,)), ((), ()))
MESH = pl.DeviceIdType.MESH
ORDER = (3, 1, 2)


def dot(a, b):
    return jnp.dot(a, b, preferred_element_type=f32)


def dot_nt(a, b):
    return lax.dot_general(a, b, NT, preferred_element_type=f32)


def halves(a):
    hi = a.astype(bf16)
    return hi, (a - hi.astype(f32)).astype(bf16)


def dot3(a, b):
    ah, al = halves(a)
    bh, bl = halves(b)
    return dot(jnp.concatenate([ah, al, ah], 1), jnp.concatenate([bh, bh, bl], 0))


def low_lanes(rows):
    return lax.broadcasted_iota(jnp.int32, (rows, 128), 1) < 64


def one_head(block, head):
    low = low_lanes(block.shape[0])
    return jnp.where(low if head % 2 == 0 else ~low, block, 0.0)


def pair_columns(array, pair):
    return array[:, pair * 128 : (pair + 1) * 128]


def softmax_terms(logits):
    return jnp.exp2(logits - jnp.max(logits, axis=1, keepdims=True))


def three_lines(level, sub):
    first = level.astype(bf16).astype(f32)
    second = (level - first).astype(bf16).astype(f32)
    third = level - first - second
    return jnp.where(
        sub == 0, first, jnp.where(sub == 1, second, jnp.where(sub == 2, third, 0.0))
    )


def kernel(
    n_seq, n_tp,
    x_hbm, w_hbm, wo_hbm, out_hbm,
    x, wk, wv, wq, wo, q, k, v, means, mk_r, qm, km, kmt,
    lv_s, lv_t, lv_m, lv_r, a_ref, z_ref, mid_r, midt, midb, e_own, outv,
    load_sem, x_sem, out_sem,
    mk_sems, lv_sems, mid_sems, mate_sems,
    wq_sems, wo_sems, km_sems, mt_sems,
):
    seq, tp = lax.axis_index("seq"), lax.axis_index("tp")
    core, chip, n_chips = lax.rem(seq, 2), lax.div(seq, 2), n_seq // 2
    n_chunks = T // C

    def rows_of(i):
        return pl.ds(pl.multiple_of(i * C, C), C)

    def to_tp(j):
        return lax.rem(tp + j, n_tp)

    def from_tp(j):
        return lax.rem(tp + n_tp - j, n_tp)

    barrier = pltpu.get_barrier_semaphore()

    loads = [
        pltpu.make_async_copy(w_hbm.at[1], wk, load_sem.at[0]),
        pltpu.make_async_copy(w_hbm.at[0], wq.at[tp], load_sem.at[1]),
        pltpu.make_async_copy(w_hbm.at[2], wv, load_sem.at[2]),
        pltpu.make_async_copy(
            wo_hbm.at[:, pl.ds(pl.multiple_of(tp * W, W), W)], wo.at[tp], load_sem.at[3]
        ),
    ]

    def x_load(i):
        return pltpu.make_async_copy(x_hbm.at[rows_of(i)], x.at[rows_of(i)], x_sem.at[i])

    loads[0].start()
    loads[1].start()
    for i in range(n_chunks):
        x_load(i).start()
    loads[2].start()
    loads[3].start()

    def peer(j):
        return {"seq": 2 * lax.rem(chip + j, n_chips) + core}

    mate = {"seq": seq + 1 - 2 * core}

    @pl.loop(1, n_chips)
    def _(j):
        pl.semaphore_signal(barrier, inc=1, device_id=peer(j), device_id_type=MESH)

    pl.semaphore_signal(barrier, inc=1, device_id=mate, device_id_type=MESH)
    for j in range(1, n_tp):
        pl.semaphore_signal(
            barrier, inc=1, device_id={"tp": to_tp(j)}, device_id_type=MESH
        )

    class Gather:
        def __init__(self, source, ref, sems):
            half = ref.shape[1] // 2
            self.source, self.ref, self.sems = source, ref, sems
            self.mine = pl.ds(pl.multiple_of(core * half, half), half)
            self.other = pl.ds(pl.multiple_of((1 - core) * half, half), half)

        def over(self, j, slot):
            return pltpu.make_async_remote_copy(
                src_ref=self.source(j, self.mine), dst_ref=self.ref.at[slot, self.mine],
                send_sem=self.sems.at[0, j], recv_sem=self.sems.at[1, j],
                device_id={"tp": to_tp(j)}, device_id_type=MESH,
            )

        def across(self, j, part):
            t = from_tp(j)
            return pltpu.make_async_remote_copy(
                src_ref=self.ref.at[t, part], dst_ref=self.ref.at[t, part],
                send_sem=self.sems.at[2, j], recv_sem=self.sems.at[3, j],
                device_id=mate, device_id_type=MESH,
            )

        def send(self):
            for j in ORDER:
                self.over(j, tp).start()

        def swap(self, j):
            self.over(j, from_tp(j)).wait_recv()
            self.across(j, self.mine).start()

        def ready(self, j):
            self.across(j, self.other).wait_recv()

        def drain(self):
            for j in ORDER:
                self.over(j, tp).wait_send()
                self.across(j, self.mine).wait_send()

    def columns_of(j):
        return pl.ds(pl.multiple_of(to_tp(j) * W, W), W)

    wq_all = Gather(lambda j, part: w_hbm.at[0, part], wq, wq_sems)
    wo_all = Gather(lambda j, part: wo_hbm.at[part, columns_of(j)], wo, wo_sems)
    km_all = Gather(lambda j, part: kmt.at[tp, part], kmt, km_sems)
    mt_all = Gather(lambda j, part: midt.at[tp, part], midt, mt_sems)

    def own_rows(i):
        x_load(i).wait()
        rows = rows_of(i)
        xc = x[rows, :]
        kp = dot(xc, wk[...])
        qp = dot(xc, wq[tp]) * LOG_SCALE
        k[rows, :] = kp.astype(bf16)
        q[tp, rows, :] = qp.astype(bf16)
        for s in range(C // SEG):
            at = i * (C // SEG) + s
            part = slice(s * SEG, (s + 1) * SEG)
            means[pl.ds(at, 1), :] = jnp.sum(qp[part], axis=0, keepdims=True) * (1.0 / SEG)
            means[pl.ds(8 + at, 1), :] = jnp.sum(kp[part], axis=0, keepdims=True) * (1.0 / SEG)

    def to_chips(src, dst, sems, j):
        return pltpu.make_async_remote_copy(
            src_ref=src, dst_ref=dst, send_sem=sems.at[0, j], recv_sem=sems.at[1, j],
            device_id=peer(j), device_id_type=MESH,
        )

    def to_mate(src, dst, n):
        return pltpu.make_async_remote_copy(
            src_ref=src, dst_ref=dst, send_sem=mate_sems.at[0, n], recv_sem=mate_sems.at[1, n],
            device_id=mate, device_id_type=MESH,
        )

    def chip_before(j):
        return lax.rem(chip + n_chips - j, n_chips)

    class Spread:
        def __init__(self, ref, sems, n):
            self.ref, self.sems, self.n = ref, sems, n

        def copy(self, j, place):
            return to_chips(self.ref.at[core, chip], self.ref.at[core, place], self.sems, j)

        def swap_copy(self, side):
            return to_mate(self.ref.at[side], self.ref.at[side], self.n)

        def send(self):
            @pl.loop(1, n_chips)
            def _(j):
                self.copy(j, chip).start()

        def swap(self):
            @pl.loop(1, n_chips)
            def _(j):
                self.copy(j, chip_before(j)).wait_recv()

            self.swap_copy(core).start()

        def ready(self):
            self.swap_copy(1 - core).wait_recv()

        def drain(self):
            @pl.loop(1, n_chips)
            def _(j):
                self.copy(j, chip).wait_send()

            self.swap_copy(core).wait_send()

    mk_all = Spread(mk_r, mk_sems, 0)
    mid_all = Spread(mid_r, mid_sems, 1)

    loads[0].wait()
    loads[1].wait()
    pl.loop(0, n_chunks)(own_rows)
    mk_r[core, chip] = means[...].astype(bf16)
    pl.semaphore_wait(barrier, n_chips + n_tp - 1)
    mk_all.send()
    wq_all.send()
    wo_all.send()

    loads[2].wait()
    ones = jnp.ones((C, 128), bf16)

    def own_values(i):
        rows = rows_of(i)
        vp = dot(x[rows, :], wv[...]).astype(bf16)
        for p in range(2):
            v[p, rows, 0:128] = pair_columns(vp, p)
            v[p, rows, 128:256] = ones

    pl.loop(0, n_chunks - 1)(own_values)
    mk_all.swap()
    own_values(n_chunks - 1)
    mk_all.ready()

    marks = mk_r[...].astype(f32).reshape(n_seq, 16, W)
    q_marks = marks[:, 0:8, :].reshape(MARKS, W)
    k_marks = marks[:, 8:16, :].reshape(MARKS, W)
    kmt[tp] = k_marks.astype(bf16)
    km_all.send()
    for h in range(4):
        qm[h] = one_head(pair_columns(q_marks, h // 2), h).astype(bf16)
        km[tp * 4 + h] = one_head(pair_columns(k_marks, h // 2), h).astype(bf16)

    sub = lax.broadcasted_iota(jnp.int32, (8, W), 0)
    for p in range(2):
        parts, levels = [], []
        for i in range(2):
            s = dot_nt(qm[2 * p + i], k[:, p * 128 : (p + 1) * 128])
            top = jnp.max(s, axis=1, keepdims=True)
            r = dot(jnp.exp2(s - top).astype(bf16), v[p])
            parts.append(r[:, :128] / r[:, 128:])
            levels.append((top + jnp.log2(r[:, 128:])).T[0:8, :])
        mean_values = jnp.where(low_lanes(MARKS), parts[0], parts[1]).T
        for i, level in enumerate(levels):
            lines = three_lines(level, sub)
            for b in range(8):
                part = mean_values[i * 64 + b * 8 : i * 64 + b * 8 + 8, :]
                at = (2 * p + i) * 8 + b
                lv_s[at // n_chips, at % n_chips] = jnp.concatenate([part, lines], 0).astype(bf16)

    lv_mate = to_mate(lv_s.at[1 - core], lv_t, 2)
    lv_mate.start()
    wq_all.swap(ORDER[0])
    for j in ORDER:
        km_all.swap(j)

    def lv_copy(j, place):
        return to_chips(lv_m.at[lax.rem(chip + j, n_chips)], lv_r.at[place], lv_sems, j)

    def merged(blocks):
        level = blocks[:, 8:9, :] + blocks[:, 9:10, :] + blocks[:, 10:11, :]
        top = jnp.max(level, axis=0, keepdims=True)
        share = jnp.exp2(level - top)
        total = jnp.sum(share, axis=0)
        return jnp.sum(blocks[:, 0:8, :] * share, axis=0) / total, top[0] + jnp.log2(total)

    head = 2 * core + lax.div(chip, 8)
    terms = softmax_terms(dot_nt(qm[head], km[tp * 4 + head]))
    kernel_a = terms / jnp.sum(terms, axis=1, keepdims=True)
    col = jnp.max(jnp.sum(kernel_a, axis=0, keepdims=True), axis=1, keepdims=True)
    row = jnp.max(jnp.sum(kernel_a, axis=1, keepdims=True), axis=0, keepdims=True)
    a_ref[...] = kernel_a
    z_ref[...] = kernel_a.T / (col * row)
    wq_all.ready(ORDER[0])

    def unit(u):
        g = lax.div(u, 16)
        t = lax.rem(tp + 1 + 2 * g + lax.div(g, 2), n_tp)
        rows = pl.ds(pl.multiple_of(lax.rem(u, 16) * 256, 256), 256)
        q[t, rows, :] = (dot(x[rows, :], wq[t]) * LOG_SCALE).astype(bf16)

    def newton_turn(turn):
        eye = jnp.where(
            lax.broadcasted_iota(jnp.int32, (MARKS, MARKS), 0)
            == lax.broadcasted_iota(jnp.int32, (MARKS, MARKS), 1),
            1.0,
            0.0,
        )
        first = turn * UNITS
        z = z_ref[...]
        az = dot3(a_ref[...], z)
        unit(first)
        unit(first + 1)
        inner = dot3(az, 7.0 * eye - az)
        unit(first + 2)
        unit(first + 3)
        outer = dot3(az, 15.0 * eye - inner)
        unit(first + 4)
        unit(first + 5)
        z_ref[...] = 0.25 * dot3(z, 13.0 * eye - outer)
        unit(first + 6)

    newton_turn(0)
    lv_mate.wait_recv()
    for c in range(n_chips):
        values, level = merged(jnp.stack([lv_s[core, c].astype(f32), lv_t[c].astype(f32)]))
        lines = three_lines(jnp.broadcast_to(level, (8, MARKS)), sub)
        lv_m[c] = jnp.concatenate([values, lines], 0).astype(bf16)
    @pl.loop(1, n_chips)
    def _(j):
        lv_copy(j, chip).start()

    lv_r[chip] = lv_m[chip]
    newton_turn(1)
    for j in ORDER[1:]:
        wq_all.swap(j)
    for j in ORDER:
        wo_all.swap(j)
    for j in ORDER[1:]:
        wq_all.ready(j)
    pl.loop(2, NEWTON)(newton_turn)

    @pl.loop(1, n_chips)
    def _(j):
        lv_copy(j, chip_before(j)).wait_recv()

    columns, _ = merged(lv_r[...].astype(f32))
    ch, cl = halves(columns)
    zh, zl = halves(z_ref[...])
    mid_r[core, chip] = dot_nt(
        jnp.concatenate([ch, cl, ch], 1), jnp.concatenate([zh, zh, zl], 1)
    )
    mid_all.send()

    @pl.loop(0, n_chunks)
    def _(i):
        rows = rows_of(i)
        for h in range(4):
            p = h // 2
            logits = dot_nt(q[tp, rows, p * 128 : (p + 1) * 128], km[tp * 4 + h])
            e_own[rows, h * MARKS : (h + 1) * MARKS] = softmax_terms(logits).astype(bf16)

    mid_all.swap()
    pl.loop(UNITS * NEWTON, 48)(unit)
    for j in ORDER:
        t = from_tp(j)
        km_all.ready(j)
        others = kmt[t].astype(f32)
        for h in range(4):
            km[t * 4 + h] = one_head(pair_columns(others, h // 2), h).astype(bf16)
    mid_all.ready()

    def place_middle(t):
        m = midt[t].astype(f32)
        low = low_lanes(MARKS)
        for p in range(2):
            both = pair_columns(m, p)
            for i in range(2):
                mask = low if i == 0 else ~low
                midb[t * 2 + p, i * MARKS : (i + 1) * MARKS, :] = jnp.concatenate(
                    [jnp.where(mask, both, 0.0), jnp.where(mask, 1.0, 0.0)], 1
                ).astype(bf16)

    midt[tp] = mid_r[...].reshape(W, MARKS).T.astype(bf16)
    mt_all.send()
    place_middle(tp)

    def normalised(r):
        return (r[:, :128] * (1.0 / r[:, 128:])).astype(bf16)

    def own_attended(i):
        rows = rows_of(i)
        for p in range(2):
            r = dot(e_own[rows, p * 512 : (p + 1) * 512], midb[tp * 2 + p])
            q[tp, rows, p * 128 : (p + 1) * 128] = normalised(r)

    pl.loop(0, n_chunks - 1)(own_attended)
    for j in ORDER:
        mt_all.swap(j)
    own_attended(n_chunks - 1)
    loads[3].wait()
    for j in ORDER:
        wo_all.ready(j)
        mt_all.ready(j)
        place_middle(from_tp(j))
    groups = [from_tp(j) for j in ORDER]

    def out_copy(i):
        return pltpu.make_async_copy(outv.at[rows_of(i)], out_hbm.at[rows_of(i)], out_sem.at[i])

    @pl.loop(0, n_chunks)
    def _(i):
        rows = rows_of(i)
        parts = [q[tp, rows, :]]
        for t in groups:
            for p in range(2):
                qc = q[t, rows, p * 128 : (p + 1) * 128]
                e = [
                    softmax_terms(dot_nt(qc, km[t * 4 + 2 * p + b])).astype(bf16) for b in range(2)
                ]
                parts.append(normalised(dot(jnp.concatenate(e, 1), midb[t * 2 + p])))
        weights = jnp.concatenate([wo[t] for t in [tp] + groups], 0)
        outv[rows, :] = dot(jnp.concatenate(parts, 1), weights).astype(bf16)
        out_copy(i).start()

    @pl.loop(1, n_chips)
    def _(j):
        lv_copy(j, chip).wait_send()

    lv_mate.wait_send()
    for part in (mk_all, mid_all, wq_all, wo_all, km_all, mt_all):
        part.drain()
    for i in range(n_chunks):
        out_copy(i).wait()


def on_device(n_seq, n_tp, tokens, w_qkv, w_out):
    vmem = pltpu.VMEM
    sems = pltpu.SemaphoreType.DMA
    n_chips = n_seq // 2
    scratch = [
        vmem((T, D), bf16),
        vmem((D, W), bf16),
        vmem((D, W), bf16),
        vmem((n_tp, D, W), bf16),
        vmem((n_tp, W, W), bf16),
        vmem((n_tp, T, W), bf16),
        vmem((T, W), bf16),
        vmem((2, T, 256), bf16),
        vmem((16, W), f32),
        vmem((2, n_chips, 16, W), bf16),
        vmem((4, MARKS, 128), bf16),
        vmem((4 * n_tp, MARKS, 128), bf16),
        vmem((n_tp, MARKS, W), bf16),
        vmem((2, n_chips, 16, MARKS), bf16),
        vmem((n_chips, 16, MARKS), bf16),
        vmem((n_chips, 16, MARKS), bf16),
        vmem((n_chips, 16, MARKS), bf16),
        vmem((MARKS, MARKS), f32),
        vmem((MARKS, MARKS), f32),
        vmem((2, n_chips, 8, MARKS), f32),
        vmem((n_tp, MARKS, W), bf16),
        vmem((2 * n_tp, 2 * MARKS, 256), bf16),
        vmem((T, 4 * MARKS), bf16),
        vmem((T, W), bf16),
        sems((4,)), sems((T // C,)), sems((T // C,)),
        *[sems((2, n_chips))] * 3,
        sems((2, 3)),
        *[sems((4, n_tp))] * 4,
    ]
    hbm = pl.BlockSpec(memory_space=pl.ANY)
    return pl.pallas_call(
        functools.partial(kernel, n_seq, n_tp),
        out_shape=jax.ShapeDtypeStruct((T, W), bf16),
        in_specs=[hbm] * 3,
        out_specs=hbm,
        scratch_shapes=scratch,
        compiler_params=pltpu.CompilerParams(
            collective_id=0, has_side_effects=True, vmem_limit_bytes=60 * 2**20
        ),
    )(tokens, w_qkv, w_out)


def solution(mesh):
    return jax.shard_map(
        functools.partial(on_device, mesh.shape["seq"], mesh.shape["tp"]),
        mesh=mesh,
        in_specs=(P("seq", None), P(None, None, "tp"), P("tp", None)),
        out_specs=P("seq", "tp"),
        check_vma=False,
    )
```

time: 83.5 us -> 81.8 us (0.980)
  Pallas kernels: 80.3 us -> 78.6 us
    pallas_call x1, Pallas kernels: 80.3 us -> 78.6 us  [on_device(): pl.pallas_call(functools.partial(kernel, n_seq, n_tp), out_shape=jax.Shap...]
where the time goes in v3:
time: 81.8 us; the launch traced here: 81.7 us
  Pallas kernels  78.6 us (96%)
  local copies, waits for them, and re-layouts  3.05 us (4%)
    pallas_call x1, Pallas kernels, on_device(): pl.pallas_call(functools.partial(kernel, n_seq, n_tp), out_shape=jax.Shap...  78.6 us
    unnamed x1, local copies, waits for them, and re-layouts  3.05 us

profile of v3, /device:TPU:1, one launch (start us, length us, event | category | flops | bytes accessed | tf_op | source)
XLA Modules:
  0.0 81.7 jit_solution(9850924956810987112)
XLA Ops:
  0.0 78.6 %shard_map.37 = bf16[4096,256]{1,0:T(8,128)(2,1)} custom-call(bf16[4096,1024]{1,0:T(8,128)(2,1)} %x_hbm.1, bf16[3,1024,256]{2,1,0:T(8,128)(2,1)} %w_hbm.1, bf16[256,1024]{1,0:T(8,128)(2,1)} %wo_hbm.1), custom_call_target="tpu_custom_call" | custom-call | tf_op jit(solution)/shard_map/pallas_call | solution.py:491
  78.6 3.0 %copy.5 = bf16[4096,256]{1,0:T(8,128)(2,1)} copy(bf16[4096,256]{1,0:T(8,128)(2,1)} %shard_map.37) | data formatting | bytes 4194304

commit v4 on v3

--- a/solution.py
+++ b/solution.py
@@ -11,7 +11,7 @@
 HEAD_DIM = 64
 MARKS = 256
 NEWTON = 6
-UNITS = 7
+UNITS = 4
 D = 1024
 W = 256
 T = 4096
@@ -296,12 +296,9 @@
     def lv_copy(j, place):
         return to_chips(lv_m.at[lax.rem(chip + j, n_chips)], lv_r.at[place], lv_sems, j)
 
-    def merged(blocks):
-        level = blocks[:, 8:9, :] + blocks[:, 9:10, :] + blocks[:, 10:11, :]
-        top = jnp.max(level, axis=0, keepdims=True)
-        share = jnp.exp2(level - top)
-        total = jnp.sum(share, axis=0)
-        return jnp.sum(blocks[:, 0:8, :] * share, axis=0) / total, top[0] + jnp.log2(total)
+    def values_and_level(blocks):
+        blocks = blocks.astype(f32)
+        return blocks[:, 0:8, :], blocks[:, 8:9, :] + blocks[:, 9:10, :] + blocks[:, 10:11, :]
 
     head = 2 * core + lax.div(chip, 8)
     terms = softmax_terms(dot_nt(qm[head], km[tp * 4 + head]))
@@ -329,41 +326,41 @@
         z = z_ref[...]
         az = dot3(a_ref[...], z)
         unit(first)
+        inner = dot3(az, 7.0 * eye - az)
         unit(first + 1)
-        inner = dot3(az, 7.0 * eye - az)
+        outer = dot3(az, 15.0 * eye - inner)
         unit(first + 2)
+        z_ref[...] = 0.25 * dot3(z, 13.0 * eye - outer)
         unit(first + 3)
-        outer = dot3(az, 15.0 * eye - inner)
-        unit(first + 4)
-        unit(first + 5)
-        z_ref[...] = 0.25 * dot3(z, 13.0 * eye - outer)
-        unit(first + 6)
 
     newton_turn(0)
     lv_mate.wait_recv()
-    for c in range(n_chips):
-        values, level = merged(jnp.stack([lv_s[core, c].astype(f32), lv_t[c].astype(f32)]))
-        lines = three_lines(jnp.broadcast_to(level, (8, MARKS)), sub)
-        lv_m[c] = jnp.concatenate([values, lines], 0).astype(bf16)
+    (va, la), (vb, lb) = values_and_level(lv_s[core]), values_and_level(lv_t[...])
+    top = jnp.maximum(la, lb)
+    wa, wb = jnp.exp2(la - top), jnp.exp2(lb - top)
+    level = jnp.broadcast_to(top + jnp.log2(wa + wb), va.shape)
+    lines = three_lines(level, lax.broadcasted_iota(jnp.int32, va.shape, 1))
+    lv_m[...] = jnp.concatenate([(va * wa + vb * wb) / (wa + wb), lines], 1).astype(bf16)
+
     @pl.loop(1, n_chips)
     def _(j):
         lv_copy(j, chip).start()
 
     lv_r[chip] = lv_m[chip]
-    newton_turn(1)
-    for j in ORDER[1:]:
-        wq_all.swap(j)
-    for j in ORDER:
-        wo_all.swap(j)
-    for j in ORDER[1:]:
-        wq_all.ready(j)
-    pl.loop(2, NEWTON)(newton_turn)
+    pl.loop(1, 3)(newton_turn)
+    wq_all.swap(ORDER[1])
+    newton_turn(3)
+    wq_all.ready(ORDER[1])
+    pl.loop(4, NEWTON)(newton_turn)
+    wq_all.swap(ORDER[2])
 
     @pl.loop(1, n_chips)
     def _(j):
         lv_copy(j, chip_before(j)).wait_recv()
 
-    columns, _ = merged(lv_r[...].astype(f32))
+    values, level = values_and_level(lv_r[...])
+    share = jnp.exp2(level - jnp.max(level, axis=0, keepdims=True))
+    columns = jnp.sum(values * share, axis=0) / jnp.sum(share, axis=0)
     ch, cl = halves(columns)
     zh, zl = halves(z_ref[...])
     mid_r[core, chip] = dot_nt(
@@ -379,8 +376,12 @@
             logits = dot_nt(q[tp, rows, p * 128 : (p + 1) * 128], km[tp * 4 + h])
             e_own[rows, h * MARKS : (h + 1) * MARKS] = softmax_terms(logits).astype(bf16)
 
+    pl.loop(24, 32)(unit)
+    wq_all.ready(ORDER[2])
     mid_all.swap()
-    pl.loop(UNITS * NEWTON, 48)(unit)
+    pl.loop(32, 40)(unit)
+    for j in ORDER:
+        wo_all.swap(j)
     for j in ORDER:
         t = from_tp(j)
         km_all.ready(j)
@@ -414,9 +415,11 @@
             q[tp, rows, p * 128 : (p + 1) * 128] = normalised(r)
 
     pl.loop(0, n_chunks - 1)(own_attended)
+    pl.loop(40, 43)(unit)
     for j in ORDER:
         mt_all.swap(j)
     own_attended(n_chunks - 1)
+    pl.loop(43, 48)(unit)
     loads[3].wait()
     for j in ORDER:
         wo_all.ready(j)

time: 81.8 us -> 79.9 us (0.977)
  Pallas kernels: 78.6 us -> 76.6 us
    pallas_call x1, Pallas kernels: 78.6 us -> 76.6 us  [on_device(): pl.pallas_call(functools.partial(kernel, n_seq, n_tp), out_shape=jax.Shap...]
where the time goes in v4:
time: 79.9 us; the launch traced here: 79.6 us
  Pallas kernels  76.6 us (96%)
  local copies, waits for them, and re-layouts  3.05 us (4%)
    pallas_call x1, Pallas kernels, on_device(): pl.pallas_call(functools.partial(kernel, n_seq, n_tp), out_shape=jax.Shap...  76.6 us
    unnamed x1, local copies, waits for them, and re-layouts  3.05 us

profile of v4, /device:TPU:1, one launch (start us, length us, event | category | flops | bytes accessed | tf_op | source)
XLA Modules:
  0.0 79.6 jit_solution(7530039637225505764)
XLA Ops:
  0.0 76.6 %shard_map.37 = bf16[4096,256]{1,0:T(8,128)(2,1)} custom-call(bf16[4096,1024]{1,0:T(8,128)(2,1)} %x_hbm.1, bf16[3,1024,256]{2,1,0:T(8,128)(2,1)} %w_hbm.1, bf16[256,1024]{1,0:T(8,128)(2,1)} %wo_hbm.1), custom_call_target="tpu_custom_call" | custom-call | tf_op jit(solution)/shard_map/pallas_call | solution.py:494
  76.6 3.0 %copy.5 = bf16[4096,256]{1,0:T(8,128)(2,1)} copy(bf16[4096,256]{1,0:T(8,128)(2,1)} %shard_map.37) | data formatting | bytes 4194304

commit v5 on v4

--- a/solution.py
+++ b/solution.py
@@ -117,11 +117,13 @@
 
     mate = {"seq": seq + 1 - 2 * core}
 
-    @pl.loop(1, n_chips)
+    def any_peer(j):
+        return {"seq": lax.rem(seq + j, n_seq)}
+
+    @pl.loop(1, n_seq)
     def _(j):
-        pl.semaphore_signal(barrier, inc=1, device_id=peer(j), device_id_type=MESH)
-
-    pl.semaphore_signal(barrier, inc=1, device_id=mate, device_id_type=MESH)
+        pl.semaphore_signal(barrier, inc=1, device_id=any_peer(j), device_id_type=MESH)
+
     for j in range(1, n_tp):
         pl.semaphore_signal(
             barrier, inc=1, device_id={"tp": to_tp(j)}, device_id_type=MESH
@@ -193,9 +195,9 @@
             device_id=peer(j), device_id_type=MESH,
         )
 
-    def to_mate(src, dst, n):
+    def to_mate(src, dst):
         return pltpu.make_async_remote_copy(
-            src_ref=src, dst_ref=dst, send_sem=mate_sems.at[0, n], recv_sem=mate_sems.at[1, n],
+            src_ref=src, dst_ref=dst, send_sem=mate_sems.at[0], recv_sem=mate_sems.at[1],
             device_id=mate, device_id_type=MESH,
         )
 
@@ -203,48 +205,41 @@
         return lax.rem(chip + n_chips - j, n_chips)
 
     class Spread:
-        def __init__(self, ref, sems, n):
-            self.ref, self.sems, self.n = ref, sems, n
+        def __init__(self, ref, sems):
+            self.ref, self.sems = ref, sems
 
         def copy(self, j, place):
-            return to_chips(self.ref.at[core, chip], self.ref.at[core, place], self.sems, j)
-
-        def swap_copy(self, side):
-            return to_mate(self.ref.at[side], self.ref.at[side], self.n)
+            return pltpu.make_async_remote_copy(
+                src_ref=self.ref.at[seq], dst_ref=self.ref.at[place],
+                send_sem=self.sems.at[0, j], recv_sem=self.sems.at[1, j],
+                device_id=any_peer(j), device_id_type=MESH,
+            )
 
         def send(self):
-            @pl.loop(1, n_chips)
+            @pl.loop(1, n_seq)
             def _(j):
-                self.copy(j, chip).start()
-
-        def swap(self):
-            @pl.loop(1, n_chips)
+                self.copy(j, seq).start()
+
+        def ready(self):
+            @pl.loop(1, n_seq)
             def _(j):
-                self.copy(j, chip_before(j)).wait_recv()
-
-            self.swap_copy(core).start()
-
-        def ready(self):
-            self.swap_copy(1 - core).wait_recv()
+                self.copy(j, lax.rem(seq + n_seq - j, n_seq)).wait_recv()
 
         def drain(self):
-            @pl.loop(1, n_chips)
+            @pl.loop(1, n_seq)
             def _(j):
-                self.copy(j, chip).wait_send()
-
-            self.swap_copy(core).wait_send()
-
-    mk_all = Spread(mk_r, mk_sems, 0)
-    mid_all = Spread(mid_r, mid_sems, 1)
+                self.copy(j, seq).wait_send()
+
+    mk_all = Spread(mk_r, mk_sems)
+    mid_all = Spread(mid_r, mid_sems)
 
     loads[0].wait()
     loads[1].wait()
     pl.loop(0, n_chunks)(own_rows)
-    mk_r[core, chip] = means[...].astype(bf16)
-    pl.semaphore_wait(barrier, n_chips + n_tp - 1)
+    mk_r[seq] = means[...].astype(bf16)
+    pl.semaphore_wait(barrier, n_seq - 1 + n_tp - 1)
     mk_all.send()
     wq_all.send()
-    wo_all.send()
 
     loads[2].wait()
     ones = jnp.ones((C, 128), bf16)
@@ -256,16 +251,14 @@
             v[p, rows, 0:128] = pair_columns(vp, p)
             v[p, rows, 128:256] = ones
 
-    pl.loop(0, n_chunks - 1)(own_values)
-    mk_all.swap()
-    own_values(n_chunks - 1)
+    pl.loop(0, n_chunks)(own_values)
     mk_all.ready()
-
-    marks = mk_r[...].astype(f32).reshape(n_seq, 16, W)
+    marks = mk_r[...].astype(f32)
     q_marks = marks[:, 0:8, :].reshape(MARKS, W)
     k_marks = marks[:, 8:16, :].reshape(MARKS, W)
     kmt[tp] = k_marks.astype(bf16)
     km_all.send()
+    wo_all.send()
     for h in range(4):
         qm[h] = one_head(pair_columns(q_marks, h // 2), h).astype(bf16)
         km[tp * 4 + h] = one_head(pair_columns(k_marks, h // 2), h).astype(bf16)
@@ -287,11 +280,9 @@
                 at = (2 * p + i) * 8 + b
                 lv_s[at // n_chips, at % n_chips] = jnp.concatenate([part, lines], 0).astype(bf16)
 
-    lv_mate = to_mate(lv_s.at[1 - core], lv_t, 2)
+    lv_mate = to_mate(lv_s.at[1 - core], lv_t)
     lv_mate.start()
     wq_all.swap(ORDER[0])
-    for j in ORDER:
-        km_all.swap(j)
 
     def lv_copy(j, place):
         return to_chips(lv_m.at[lax.rem(chip + j, n_chips)], lv_r.at[place], lv_sems, j)
@@ -363,9 +354,7 @@
     columns = jnp.sum(values * share, axis=0) / jnp.sum(share, axis=0)
     ch, cl = halves(columns)
     zh, zl = halves(z_ref[...])
-    mid_r[core, chip] = dot_nt(
-        jnp.concatenate([ch, cl, ch], 1), jnp.concatenate([zh, zh, zl], 1)
-    )
+    mid_r[seq] = dot_nt(jnp.concatenate([ch, cl, ch], 1), jnp.concatenate([zh, zh, zl], 1))
     mid_all.send()
 
     @pl.loop(0, n_chunks)
@@ -376,18 +365,12 @@
             logits = dot_nt(q[tp, rows, p * 128 : (p + 1) * 128], km[tp * 4 + h])
             e_own[rows, h * MARKS : (h + 1) * MARKS] = softmax_terms(logits).astype(bf16)
 
-    pl.loop(24, 32)(unit)
     wq_all.ready(ORDER[2])
-    mid_all.swap()
-    pl.loop(32, 40)(unit)
+    pl.loop(24, 40)(unit)
+    for j in ORDER:
+        km_all.swap(j)
     for j in ORDER:
         wo_all.swap(j)
-    for j in ORDER:
-        t = from_tp(j)
-        km_all.ready(j)
-        others = kmt[t].astype(f32)
-        for h in range(4):
-            km[t * 4 + h] = one_head(pair_columns(others, h // 2), h).astype(bf16)
     mid_all.ready()
 
     def place_middle(t):
@@ -401,7 +384,8 @@
                     [jnp.where(mask, both, 0.0), jnp.where(mask, 1.0, 0.0)], 1
                 ).astype(bf16)
 
-    midt[tp] = mid_r[...].reshape(W, MARKS).T.astype(bf16)
+    pieces = [mid_r[2 * (n % n_chips) + n // n_chips] for n in range(n_seq)]
+    midt[tp] = jnp.concatenate(pieces, 0).T.astype(bf16)
     mt_all.send()
     place_middle(tp)
 
@@ -420,6 +404,12 @@
         mt_all.swap(j)
     own_attended(n_chunks - 1)
     pl.loop(43, 48)(unit)
+    for j in ORDER:
+        t = from_tp(j)
+        km_all.ready(j)
+        others = kmt[t].astype(f32)
+        for h in range(4):
+            km[t * 4 + h] = one_head(pair_columns(others, h // 2), h).astype(bf16)
     loads[3].wait()
     for j in ORDER:
         wo_all.ready(j)
@@ -470,7 +460,7 @@
         vmem((T, W), bf16),
         vmem((2, T, 256), bf16),
         vmem((16, W), f32),
-        vmem((2, n_chips, 16, W), bf16),
+        vmem((n_seq, 16, W), bf16),
         vmem((4, MARKS, 128), bf16),
         vmem((4 * n_tp, MARKS, 128), bf16),
         vmem((n_tp, MARKS, W), bf16),
@@ -480,14 +470,14 @@
         vmem((n_chips, 16, MARKS), bf16),
         vmem((MARKS, MARKS), f32),
         vmem((MARKS, MARKS), f32),
-        vmem((2, n_chips, 8, MARKS), f32),
+        vmem((n_seq, 8, MARKS), f32),
         vmem((n_tp, MARKS, W), bf16),
         vmem((2 * n_tp, 2 * MARKS, 256), bf16),
         vmem((T, 4 * MARKS), bf16),
         vmem((T, W), bf16),
         sems((4,)), sems((T // C,)), sems((T // C,)),
-        *[sems((2, n_chips))] * 3,
-        sems((2, 3)),
+        sems((2, n_seq)), sems((2, n_chips)), sems((2, n_seq)),
+        sems((2,)),
         *[sems((4, n_tp))] * 4,
     ]
     hbm = pl.BlockSpec(memory_space=pl.ANY)

time: 79.9 us -> 77.1 us (0.965)
  Pallas kernels: 76.6 us -> 73.9 us
    pallas_call x1, Pallas kernels: 76.6 us -> 73.9 us  [on_device(): pl.pallas_call(functools.partial(kernel, n_seq, n_tp), out_shape=jax.Shap...]
where the time goes in v5:
time: 77.1 us; the launch traced here: 77 us
  Pallas kernels  73.9 us (96%)
  local copies, waits for them, and re-layouts  3.05 us (4%)
    pallas_call x1, Pallas kernels, on_device(): pl.pallas_call(functools.partial(kernel, n_seq, n_tp), out_shape=jax.Shap...  73.9 us
    unnamed x1, local copies, waits for them, and re-layouts  3.05 us

profile of v5, /device:TPU:1, one launch (start us, length us, event | category | flops | bytes accessed | tf_op | source)
XLA Modules:
  0.0 77.0 jit_solution(1466033142087585082)
XLA Ops:
  0.0 73.9 %shard_map.37 = bf16[4096,256]{1,0:T(8,128)(2,1)} custom-call(bf16[4096,1024]{1,0:T(8,128)(2,1)} %x_hbm.1, bf16[3,1024,256]{2,1,0:T(8,128)(2,1)} %w_hbm.1, bf16[256,1024]{1,0:T(8,128)(2,1)} %wo_hbm.1), custom_call_target="tpu_custom_call" | custom-call | tf_op jit(solution)/shard_map/pallas_call | solution.py:484
  73.9 3.0 %copy.5 = bf16[4096,256]{1,0:T(8,128)(2,1)} copy(bf16[4096,256]{1,0:T(8,128)(2,1)} %shard_map.37) | data formatting | bytes 4194304

commit v6 on v5

--- a/solution.py
+++ b/solution.py
@@ -398,24 +398,44 @@
             r = dot(e_own[rows, p * 512 : (p + 1) * 512], midb[tp * 2 + p])
             q[tp, rows, p * 128 : (p + 1) * 128] = normalised(r)
 
-    pl.loop(0, n_chunks - 1)(own_attended)
-    pl.loop(40, 43)(unit)
-    for j in ORDER:
-        mt_all.swap(j)
-    own_attended(n_chunks - 1)
-    pl.loop(43, 48)(unit)
-    for j in ORDER:
+    def attended_of(t, rows):
+        parts = []
+        for p in range(2):
+            qc = q[t, rows, p * 128 : (p + 1) * 128]
+            e = [softmax_terms(dot_nt(qc, km[t * 4 + 2 * p + b])).astype(bf16) for b in range(2)]
+            parts.append(normalised(dot(jnp.concatenate(e, 1), midb[t * 2 + p])))
+        return parts
+
+    def place_group(j):
         t = from_tp(j)
         km_all.ready(j)
         others = kmt[t].astype(f32)
         for h in range(4):
             km[t * 4 + h] = one_head(pair_columns(others, h // 2), h).astype(bf16)
+        mt_all.ready(j)
+        place_middle(t)
+
+    groups = [from_tp(j) for j in ORDER]
+
+    def first_group(i):
+        rows = rows_of(i)
+        q[groups[0], rows, :] = jnp.concatenate(attended_of(groups[0], rows), 1)
+
+    pl.loop(0, n_chunks - 1)(own_attended)
+    pl.loop(40, 43)(unit)
+    mt_all.swap(ORDER[0])
+    own_attended(n_chunks - 1)
+    pl.loop(43, 48)(unit)
+    place_group(ORDER[0])
+    pl.loop(0, n_chunks // 2)(first_group)
+    for j in ORDER[1:]:
+        mt_all.swap(j)
+    pl.loop(n_chunks // 2, n_chunks)(first_group)
+    for j in ORDER[1:]:
+        place_group(j)
     loads[3].wait()
     for j in ORDER:
         wo_all.ready(j)
-        mt_all.ready(j)
-        place_middle(from_tp(j))
-    groups = [from_tp(j) for j in ORDER]
 
     def out_copy(i):
         return pltpu.make_async_copy(outv.at[rows_of(i)], out_hbm.at[rows_of(i)], out_sem.at[i])
@@ -423,14 +443,9 @@
     @pl.loop(0, n_chunks)
     def _(i):
         rows = rows_of(i)
-        parts = [q[tp, rows, :]]
-        for t in groups:
-            for p in range(2):
-                qc = q[t, rows, p * 128 : (p + 1) * 128]
-                e = [
-                    softmax_terms(dot_nt(qc, km[t * 4 + 2 * p + b])).astype(bf16) for b in range(2)
-                ]
-                parts.append(normalised(dot(jnp.concatenate(e, 1), midb[t * 2 + p])))
+        parts = [q[tp, rows, :], q[groups[0], rows, :]]
+        for t in groups[1:]:
+            parts += attended_of(t, rows)
         weights = jnp.concatenate([wo[t] for t in [tp] + groups], 0)
         outv[rows, :] = dot(jnp.concatenate(parts, 1), weights).astype(bf16)
         out_copy(i).start()

time: 77.1 us -> 75.5 us (0.979)
  Pallas kernels: 73.9 us -> 72.3 us
    pallas_call x1, Pallas kernels: 73.9 us -> 72.3 us  [on_device(): pl.pallas_call(functools.partial(kernel, n_seq, n_tp), out_shape=jax.Shap...]
where the time goes in v6:
time: 75.5 us; the launch traced here: 75.4 us
  Pallas kernels  72.3 us (96%)
  local copies, waits for them, and re-layouts  3.05 us (4%)
    pallas_call x1, Pallas kernels, on_device(): pl.pallas_call(functools.partial(kernel, n_seq, n_tp), out_shape=jax.Shap...  72.3 us
    unnamed x1, local copies, waits for them, and re-layouts  3.05 us

profile of v6, /device:TPU:1, one launch (start us, length us, event | category | flops | bytes accessed | tf_op | source)
XLA Modules:
  0.0 75.4 jit_solution(4268029242323117971)
XLA Ops:
  0.0 72.3 %shard_map.37 = bf16[4096,256]{1,0:T(8,128)(2,1)} custom-call(bf16[4096,1024]{1,0:T(8,128)(2,1)} %x_hbm.1, bf16[3,1024,256]{2,1,0:T(8,128)(2,1)} %w_hbm.1, bf16[256,1024]{1,0:T(8,128)(2,1)} %wo_hbm.1), custom_call_target="tpu_custom_call" | custom-call | tf_op jit(solution)/shard_map/pallas_call | solution.py:499
  72.4 3.0 %copy.5 = bf16[4096,256]{1,0:T(8,128)(2,1)} copy(bf16[4096,256]{1,0:T(8,128)(2,1)} %shard_map.37) | data formatting | bytes 4194304

commit v7 on v6

--- a/solution.py
+++ b/solution.py
@@ -17,6 +17,8 @@
 T = 4096
 SEG = 512
 C = 1024
+SHARE = 256
+PER_GROUP = 1 + (T - C) // 256
 LOG_SCALE = HEAD_DIM**-0.5 * math.log2(math.e)
 bf16, f32 = jnp.bfloat16, jnp.float32
 NT = (((1,), (1,)), ((), ()))
@@ -73,10 +75,10 @@
     n_seq, n_tp,
     x_hbm, w_hbm, wo_hbm, out_hbm,
     x, wk, wv, wq, wo, q, k, v, means, mk_r, qm, km, kmt,
-    lv_s, lv_t, lv_m, lv_r, a_ref, z_ref, mid_r, midt, midb, e_own, outv,
+    lv_s, lv_t, lv_m, lv_r, a_ref, z_ref, mid_r, midt, midb, e_own, outv, sent,
     load_sem, x_sem, out_sem,
     mk_sems, lv_sems, mid_sems, mate_sems,
-    wq_sems, wo_sems, km_sems, mt_sems,
+    wq_sems, wo_sems, km_sems, mt_sems, share_sems,
 ):
     seq, tp = lax.axis_index("seq"), lax.axis_index("tp")
     core, chip, n_chips = lax.rem(seq, 2), lax.div(seq, 2), n_seq // 2
@@ -97,9 +99,7 @@
         pltpu.make_async_copy(w_hbm.at[1], wk, load_sem.at[0]),
         pltpu.make_async_copy(w_hbm.at[0], wq.at[tp], load_sem.at[1]),
         pltpu.make_async_copy(w_hbm.at[2], wv, load_sem.at[2]),
-        pltpu.make_async_copy(
-            wo_hbm.at[:, pl.ds(pl.multiple_of(tp * W, W), W)], wo.at[tp], load_sem.at[3]
-        ),
+        pltpu.make_async_copy(wo_hbm, wo.at[tp], load_sem.at[3]),
     ]
 
     def x_load(i):
@@ -167,11 +167,14 @@
                 self.over(j, tp).wait_send()
                 self.across(j, self.mine).wait_send()
 
-    def columns_of(j):
-        return pl.ds(pl.multiple_of(to_tp(j) * W, W), W)
+    def columns_of(t):
+        return pl.ds(pl.multiple_of(t * W, W), W)
+
+    def share_of(t):
+        return pl.ds(pl.multiple_of(t * SHARE, SHARE), SHARE)
 
     wq_all = Gather(lambda j, part: w_hbm.at[0, part], wq, wq_sems)
-    wo_all = Gather(lambda j, part: wo_hbm.at[part, columns_of(j)], wo, wo_sems)
+    wo_all = Gather(lambda j, part: wo_hbm.at[part], wo, wo_sems)
     km_all = Gather(lambda j, part: kmt.at[tp, part], kmt, km_sems)
     mt_all = Gather(lambda j, part: midt.at[tp, part], midt, mt_sems)
 
@@ -301,9 +304,11 @@
     wq_all.ready(ORDER[0])
 
     def unit(u):
-        g = lax.div(u, 16)
+        g, r = lax.div(u, PER_GROUP), lax.rem(u, PER_GROUP)
         t = lax.rem(tp + 1 + 2 * g + lax.div(g, 2), n_tp)
-        rows = pl.ds(pl.multiple_of(lax.rem(u, 16) * 256, 256), 256)
+        later = lax.div(r + PER_GROUP - 1, PER_GROUP)
+        start = (1 - later) * tp * SHARE + later * (C + (r - 1) * 256)
+        rows = pl.ds(pl.multiple_of(start, 256), 256)
         q[t, rows, :] = (dot(x[rows, :], wq[t]) * LOG_SCALE).astype(bf16)
 
     def newton_turn(turn):
@@ -338,11 +343,11 @@
         lv_copy(j, chip).start()
 
     lv_r[chip] = lv_m[chip]
-    pl.loop(1, 3)(newton_turn)
+    newton_turn(1)
     wq_all.swap(ORDER[1])
-    newton_turn(3)
+    newton_turn(2)
     wq_all.ready(ORDER[1])
-    pl.loop(4, NEWTON)(newton_turn)
+    pl.loop(3, NEWTON)(newton_turn)
     wq_all.swap(ORDER[2])
 
     @pl.loop(1, n_chips)
@@ -357,16 +362,23 @@
     mid_r[seq] = dot_nt(jnp.concatenate([ch, cl, ch], 1), jnp.concatenate([zh, zh, zl], 1))
     mid_all.send()
 
-    @pl.loop(0, n_chunks)
-    def _(i):
-        rows = rows_of(i)
+    own_share = share_of(tp)
+
+    def own_terms(rows):
         for h in range(4):
             p = h // 2
             logits = dot_nt(q[tp, rows, p * 128 : (p + 1) * 128], km[tp * 4 + h])
             e_own[rows, h * MARKS : (h + 1) * MARKS] = softmax_terms(logits).astype(bf16)
 
+    def chunks(first, last, work):
+        @pl.loop(first, last)
+        def _(i):
+            work(rows_of(i))
+
+    chunks(1, n_chunks, own_terms)
+    own_terms(own_share)
     wq_all.ready(ORDER[2])
-    pl.loop(24, 40)(unit)
+    pl.loop(24, 36)(unit)
     for j in ORDER:
         km_all.swap(j)
     for j in ORDER:
@@ -392,8 +404,7 @@
     def normalised(r):
         return (r[:, :128] * (1.0 / r[:, 128:])).astype(bf16)
 
-    def own_attended(i):
-        rows = rows_of(i)
+    def own_attended(rows):
         for p in range(2):
             r = dot(e_own[rows, p * 512 : (p + 1) * 512], midb[tp * 2 + p])
             q[tp, rows, p * 128 : (p + 1) * 128] = normalised(r)
@@ -417,20 +428,20 @@
 
     groups = [from_tp(j) for j in ORDER]
 
-    def first_group(i):
-        rows = rows_of(i)
+    def first_group(rows):
         q[groups[0], rows, :] = jnp.concatenate(attended_of(groups[0], rows), 1)
 
-    pl.loop(0, n_chunks - 1)(own_attended)
-    pl.loop(40, 43)(unit)
+    chunks(1, n_chunks - 1, own_attended)
+    pl.loop(36, 3 * PER_GROUP)(unit)
     mt_all.swap(ORDER[0])
-    own_attended(n_chunks - 1)
-    pl.loop(43, 48)(unit)
+    chunks(n_chunks - 1, n_chunks, own_attended)
+    own_attended(own_share)
     place_group(ORDER[0])
-    pl.loop(0, n_chunks // 2)(first_group)
+    chunks(1, n_chunks - 1, first_group)
     for j in ORDER[1:]:
         mt_all.swap(j)
-    pl.loop(n_chunks // 2, n_chunks)(first_group)
+    chunks(n_chunks - 1, n_chunks, first_group)
+    first_group(own_share)
     for j in ORDER[1:]:
         place_group(j)
     loads[3].wait()
@@ -440,15 +451,41 @@
     def out_copy(i):
         return pltpu.make_async_copy(outv.at[rows_of(i)], out_hbm.at[rows_of(i)], out_sem.at[i])
 
-    @pl.loop(0, n_chunks)
-    def _(i):
-        rows = rows_of(i)
+    def all_attended(rows):
         parts = [q[tp, rows, :], q[groups[0], rows, :]]
         for t in groups[1:]:
             parts += attended_of(t, rows)
-        weights = jnp.concatenate([wo[t] for t in [tp] + groups], 0)
-        outv[rows, :] = dot(jnp.concatenate(parts, 1), weights).astype(bf16)
+        return jnp.concatenate(parts, 1)
+
+    def out_columns(attended, t):
+        columns = columns_of(t)
+        weights = jnp.concatenate([wo[g, :, columns] for g in [tp] + groups], 0)
+        return dot(attended, weights).astype(bf16)
+
+    def share_copy(j, t):
+        return pltpu.make_async_remote_copy(
+            src_ref=sent.at[j], dst_ref=outv.at[share_of(t)],
+            send_sem=share_sems.at[0, j], recv_sem=share_sems.at[1, j],
+            device_id={"tp": to_tp(j)}, device_id_type=MESH,
+        )
+
+    attended = all_attended(own_share)
+    for j in (2, 1, 3):
+        sent[j] = out_columns(attended, to_tp(j))
+        share_copy(j, tp).start()
+    outv[own_share, :] = out_columns(attended, tp)
+
+    @pl.loop(1, n_chunks)
+    def _(i):
+        rows = rows_of(i)
+        outv[rows, :] = out_columns(all_attended(rows), tp)
         out_copy(i).start()
+
+    for j in ORDER:
+        share_copy(j, from_tp(j)).wait_recv()
+    out_copy(0).start()
+    for j in ORDER:
+        share_copy(j, tp).wait_send()
 
     @pl.loop(1, n_chips)
     def _(j):
@@ -470,7 +507,7 @@
         vmem((D, W), bf16),
         vmem((D, W), bf16),
         vmem((n_tp, D, W), bf16),
-        vmem((n_tp, W, W), bf16),
+        vmem((n_tp, W, D), bf16),
         vmem((n_tp, T, W), bf16),
         vmem((T, W), bf16),
         vmem((2, T, 256), bf16),
@@ -490,10 +527,12 @@
         vmem((2 * n_tp, 2 * MARKS, 256), bf16),
         vmem((T, 4 * MARKS), bf16),
         vmem((T, W), bf16),
+        vmem((n_tp, SHARE, W), bf16),
         sems((4,)), sems((T // C,)), sems((T // C,)),
         sems((2, n_seq)), sems((2, n_chips)), sems((2, n_seq)),
         sems((2,)),
         *[sems((4, n_tp))] * 4,
+        sems((2, n_tp)),
     ]
     hbm = pl.BlockSpec(memory_space=pl.ANY)
     return pl.pallas_call(

time: 75.5 us -> 72.6 us (0.962)
  Pallas kernels: 72.3 us -> 69.4 us
    pallas_call x1, Pallas kernels: 72.3 us -> 69.4 us  [on_device(): pl.pallas_call(functools.partial(kernel, n_seq, n_tp), out_shape=jax.Shap...]
where the time goes in v7:
time: 72.6 us; the launch traced here: 72.5 us
  Pallas kernels  69.4 us (96%)
  local copies, waits for them, and re-layouts  3.05 us (4%)
    pallas_call x1, Pallas kernels, on_device(): pl.pallas_call(functools.partial(kernel, n_seq, n_tp), out_shape=jax.Shap...  69.4 us
    unnamed x1, local copies, waits for them, and re-layouts  3.05 us

profile of v7, /device:TPU:1, one launch (start us, length us, event | category | flops | bytes accessed | tf_op | source)
XLA Modules:
  0.0 72.5 jit_solution(12466969224111337028)
XLA Ops:
  0.0 69.4 %shard_map.37 = bf16[4096,256]{1,0:T(8,128)(2,1)} custom-call(bf16[4096,1024]{1,0:T(8,128)(2,1)} %x_hbm.1, bf16[3,1024,256]{2,1,0:T(8,128)(2,1)} %w_hbm.1, bf16[256,1024]{1,0:T(8,128)(2,1)} %wo_hbm.1), custom_call_target="tpu_custom_call" | custom-call | tf_op jit(solution)/shard_map/pallas_call | solution.py:538
  69.4 3.0 %copy.5 = bf16[4096,256]{1,0:T(8,128)(2,1)} copy(bf16[4096,256]{1,0:T(8,128)(2,1)} %shard_map.37) | data formatting | bytes 4194304

commit v8 on v7

--- a/solution.py
+++ b/solution.py
@@ -26,6 +26,13 @@
 ORDER = (3, 1, 2)
 
 
+RING = 4
+OFFSETS = sorted(
+    ((dz, dx, dc) for dz in range(RING) for dx in range(RING) for dc in range(2) if dz or dx or dc),
+    key=lambda o: -(min(o[0], RING - o[0]) + min(o[1], RING - o[1])),
+)
+
+
 def dot(a, b):
     return jnp.dot(a, b, preferred_element_type=f32)
 
@@ -117,13 +124,22 @@
 
     mate = {"seq": seq + 1 - 2 * core}
 
-    def any_peer(j):
-        return {"seq": lax.rem(seq + j, n_seq)}
-
-    @pl.loop(1, n_seq)
-    def _(j):
-        pl.semaphore_signal(barrier, inc=1, device_id=any_peer(j), device_id_type=MESH)
-
+    zs = [lax.rem(lax.div(chip, RING) + d, RING) for d in range(RING)]
+    xs = [lax.rem(lax.rem(chip, RING) + d, RING) for d in range(RING)]
+    cores = [core, 1 - core]
+
+    def ahead(offset):
+        dz, dx, dc = offset
+        return (zs[dz] * RING + xs[dx]) * 2 + cores[dc]
+
+    def behind(offset):
+        dz, dx, dc = offset
+        return ahead(((RING - dz) % RING, (RING - dx) % RING, dc))
+
+    for offset in OFFSETS:
+        pl.semaphore_signal(
+            barrier, inc=1, device_id={"seq": ahead(offset)}, device_id_type=MESH
+        )
     for j in range(1, n_tp):
         pl.semaphore_signal(
             barrier, inc=1, device_id={"tp": to_tp(j)}, device_id_type=MESH
@@ -211,27 +227,25 @@
         def __init__(self, ref, sems):
             self.ref, self.sems = ref, sems
 
-        def copy(self, j, place):
+        def copy(self, offset, place):
+            j = (offset[0] * RING + offset[1]) * 2 + offset[2]
             return pltpu.make_async_remote_copy(
                 src_ref=self.ref.at[seq], dst_ref=self.ref.at[place],
                 send_sem=self.sems.at[0, j], recv_sem=self.sems.at[1, j],
-                device_id=any_peer(j), device_id_type=MESH,
+                device_id={"seq": ahead(offset)}, device_id_type=MESH,
             )
 
         def send(self):
-            @pl.loop(1, n_seq)
-            def _(j):
-                self.copy(j, seq).start()
+            for offset in OFFSETS:
+                self.copy(offset, seq).start()
 
         def ready(self):
-            @pl.loop(1, n_seq)
-            def _(j):
-                self.copy(j, lax.rem(seq + n_seq - j, n_seq)).wait_recv()
+            for offset in OFFSETS:
+                self.copy(offset, behind(offset)).wait_recv()
 
         def drain(self):
-            @pl.loop(1, n_seq)
-            def _(j):
-                self.copy(j, seq).wait_send()
+            for offset in OFFSETS:
+                self.copy(offset, seq).wait_send()
 
     mk_all = Spread(mk_r, mk_sems)
     mid_all = Spread(mid_r, mid_sems)

time: 72.6 us -> 72.7 us (level)
  no operation moved by 1% of the time
where the time goes in v8:
time: 72.7 us; the launch traced here: 72.6 us
  Pallas kernels  69.5 us (96%)
  local copies, waits for them, and re-layouts  3.05 us (4%)
    pallas_call x1, Pallas kernels, on_device(): pl.pallas_call(functools.partial(kernel, n_seq, n_tp), out_shape=jax.Shap...  69.5 us
    unnamed x1, local copies, waits for them, and re-layouts  3.05 us

profile of v8, /device:TPU:1, one launch (start us, length us, event | category | flops | bytes accessed | tf_op | source)
XLA Modules:
  0.0 72.6 jit_solution(8687334953382051609)
XLA Ops:
  0.0 69.5 %shard_map.37 = bf16[4096,256]{1,0:T(8,128)(2,1)} custom-call(bf16[4096,1024]{1,0:T(8,128)(2,1)} %x_hbm.1, bf16[3,1024,256]{2,1,0:T(8,128)(2,1)} %w_hbm.1, bf16[256,1024]{1,0:T(8,128)(2,1)} %wo_hbm.1), custom_call_target="tpu_custom_call" | custom-call | tf_op jit(solution)/shard_map/pallas_call | solution.py:552
  69.5 3.0 %copy.5 = bf16[4096,256]{1,0:T(8,128)(2,1)} copy(bf16[4096,256]{1,0:T(8,128)(2,1)} %shard_map.37) | data formatting | bytes 4194304

commit v9 on v7

--- a/solution.py
+++ b/solution.py
@@ -359,7 +359,8 @@
     columns = jnp.sum(values * share, axis=0) / jnp.sum(share, axis=0)
     ch, cl = halves(columns)
     zh, zl = halves(z_ref[...])
-    mid_r[seq] = dot_nt(jnp.concatenate([ch, cl, ch], 1), jnp.concatenate([zh, zh, zl], 1))
+    middle = dot_nt(jnp.concatenate([ch, cl, ch], 1), jnp.concatenate([zh, zh, zl], 1))
+    mid_r[seq] = jnp.concatenate([middle[:, :128], middle[:, 128:]], 0).astype(bf16)
     mid_all.send()
 
     own_share = share_of(tp)
@@ -396,8 +397,9 @@
                     [jnp.where(mask, both, 0.0), jnp.where(mask, 1.0, 0.0)], 1
                 ).astype(bf16)
 
-    pieces = [mid_r[2 * (n % n_chips) + n // n_chips] for n in range(n_seq)]
-    midt[tp] = jnp.concatenate(pieces, 0).T.astype(bf16)
+    pieces = [mid_r[2 * (n % n_chips) + n // n_chips].astype(f32) for n in range(n_seq)]
+    lines = [jnp.concatenate([piece[0:8], piece[8:16]], 1) for piece in pieces]
+    midt[tp] = jnp.concatenate(lines, 0).T.astype(bf16)
     mt_all.send()
     place_middle(tp)
 
@@ -522,7 +524,7 @@
         vmem((n_chips, 16, MARKS), bf16),
         vmem((MARKS, MARKS), f32),
         vmem((MARKS, MARKS), f32),
-        vmem((n_seq, 8, MARKS), f32),
+        vmem((n_seq, 16, MARKS // 2), bf16),
         vmem((n_tp, MARKS, W), bf16),
         vmem((2 * n_tp, 2 * MARKS, 256), bf16),
         vmem((T, 4 * MARKS), bf16),

time: 72.6 us -> 72.3 us (level)
  no operation moved by 1% of the time
where the time goes in v9:
time: 72.3 us; the launch traced here: 72.2 us
  Pallas kernels  69.1 us (96%)
  local copies, waits for them, and re-layouts  3.05 us (4%)
    pallas_call x1, Pallas kernels, on_device(): pl.pallas_call(functools.partial(kernel, n_seq, n_tp), out_shape=jax.Shap...  69.1 us
    unnamed x1, local copies, waits for them, and re-layouts  3.05 us

profile of v9, /device:TPU:1, one launch (start us, length us, event | category | flops | bytes accessed | tf_op | source)
XLA Modules:
  0.0 72.2 jit_solution(8531286750336547281)
XLA Ops:
  0.0 69.1 %shard_map.37 = bf16[4096,256]{1,0:T(8,128)(2,1)} custom-call(bf16[4096,1024]{1,0:T(8,128)(2,1)} %x_hbm.1, bf16[3,1024,256]{2,1,0:T(8,128)(2,1)} %w_hbm.1, bf16[256,1024]{1,0:T(8,128)(2,1)} %wo_hbm.1), custom_call_target="tpu_custom_call" | custom-call | tf_op jit(solution)/shard_map/pallas_call | solution.py:540
  69.1 3.0 %copy.5 = bf16[4096,256]{1,0:T(8,128)(2,1)} copy(bf16[4096,256]{1,0:T(8,128)(2,1)} %shard_map.37) | data formatting | bytes 4194304

commit v10 on v7

--- a/solution.py
+++ b/solution.py
@@ -437,11 +437,11 @@
     chunks(n_chunks - 1, n_chunks, own_attended)
     own_attended(own_share)
     place_group(ORDER[0])
-    chunks(1, n_chunks - 1, first_group)
+    first_group(own_share)
+    chunks(1, 2, first_group)
     for j in ORDER[1:]:
         mt_all.swap(j)
-    chunks(n_chunks - 1, n_chunks, first_group)
-    first_group(own_share)
+    chunks(2, n_chunks - 1, first_group)
     for j in ORDER[1:]:
         place_group(j)
     loads[3].wait()
@@ -474,6 +474,7 @@
         sent[j] = out_columns(attended, to_tp(j))
         share_copy(j, tp).start()
     outv[own_share, :] = out_columns(attended, tp)
+    chunks(n_chunks - 1, n_chunks, first_group)
 
     @pl.loop(1, n_chunks)
     def _(i):

time: 72.6 us -> 72.4 us (level)
  no operation moved by 1% of the time
where the time goes in v10:
time: 72.4 us; the launch traced here: 72.2 us
  Pallas kernels  69.2 us (96%)
  local copies, waits for them, and re-layouts  3.05 us (4%)
    pallas_call x1, Pallas kernels, on_device(): pl.pallas_call(functools.partial(kernel, n_seq, n_tp), out_shape=jax.Shap...  69.2 us
    unnamed x1, local copies, waits for them, and re-layouts  3.05 us

profile of v10, /device:TPU:1, one launch (start us, length us, event | category | flops | bytes accessed | tf_op | source)
XLA Modules:
  0.0 72.2 jit_solution(7205329313593656511)
XLA Ops:
  0.0 69.2 %shard_map.37 = bf16[4096,256]{1,0:T(8,128)(2,1)} custom-call(bf16[4096,1024]{1,0:T(8,128)(2,1)} %x_hbm.1, bf16[3,1024,256]{2,1,0:T(8,128)(2,1)} %w_hbm.1, bf16[256,1024]{1,0:T(8,128)(2,1)} %wo_hbm.1), custom_call_target="tpu_custom_call" | custom-call | tf_op jit(solution)/shard_map/pallas_call | solution.py:539
  69.2 3.0 %copy.5 = bf16[4096,256]{1,0:T(8,128)(2,1)} copy(bf16[4096,256]{1,0:T(8,128)(2,1)} %shard_map.37) | data formatting | bytes 4194304
